TPU v7x, 32 devices: a whole 2x2x4 slice. The times are simulated.
32 devices in a mesh: replica: 16 (over z, y, core), shard: 2 (over x).
Axes of the slice: x: 2, y: 2, z: 4, core: 2. Of those that a mesh axis runs over, the one named last changes fastest.
Arguments:
- tokens: bfloat16 [8192, 768], P(('replica', 'shard')), may hold values from -6 to 6
- cotangent: bfloat16 [8192, 768], P(('replica', 'shard')), may hold values from -6 to 6
- positions: int32 [8192], P(('replica', 'shard')), may hold values from 0 to 1023, as said below
- rest: int32 [8192], P(('replica', 'shard')), may hold values from 0 to 1023, as said below
- first_gain: bfloat16 [768], P('shard'), may hold values from 0.25 to 1.75
- second_gain: bfloat16 [768], P('shard'), may hold values from 0.25 to 1.75
- merged_weight: bfloat16 [768, 2304], P('shard'), may hold values from -0.21875 to 0.21875
- output_weight: bfloat16 [768, 768], P('shard'), may hold values from -0.875 to 0.875
- input_weight: bfloat16 [768, 2304], P('shard'), may hold values from -0.21875 to 0.21875
- down_weight: bfloat16 [1152, 768], P('shard'), may hold values from -0.1875 to 0.1875
Outputs:
- mixed: bfloat16 [8192, 768], P(('replica', 'shard'))
- token_grad: float32 [8192, 768], P(('replica', 'shard'))
- first_gain_grad: float32 [768], P('shard')
- second_gain_grad: float32 [768], P('shard')
- merged_grad: float32 [768, 2304], P('shard')
- output_grad: float32 [768, 768], P('shard')
- input_grad: float32 [768, 2304], P('shard')
- down_grad: float32 [1152, 768], P('shard')
Inputs may be any that keep to these rules, and one draw needn't show every extreme that they name: Documents are packed end to end, the first entered part way: positions[t + 1] = positions[t] + 1 and rest[t + 1] = rest[t] - 1 inside a document, and where rest[t] = 0 the next token starts a new document with position 0. Every document has 512 to 1024 tokens (the first and last may be cut by the ends), and one has exactly 1024. rest[t] + positions[t] + 1 is the length of t's document.
All inputs are finite; a program needn't handle non-finite values.
Results may differ from a plain program's by a relative error of at most 0.024.
Values may be sent and summed in bfloat16 or wider, within the bound.
A program may use at most 128 MiB of HBM per device.

v0:
```python
import math

import jax
import jax.numpy as jnp
from jax import lax
from jax.sharding import PartitionSpec as P

D = 768
HEADS = 12
HEAD_DIM = 64
FF = 1152
WINDOW = 64


EPSILON = 1e-05
NEGATIVE = -1e30


def extended(cells, sides, width):
    for axis, dim in sides:
        count = lax.axis_size(axis)
        ends = count - 1
        head = lax.slice_in_dim(cells, 0, width, axis=dim)
        tail = lax.slice_in_dim(cells, cells.shape[dim] - width, cells.shape[dim], axis=dim)
        cells = jnp.concatenate(
            [
                lax.ppermute(tail, axis, [(i, (i + 1) % count) for i in range(ends)]),
                cells,
                lax.ppermute(head, axis, [((i + 1) % count, i) for i in range(ends)]),
            ],
            axis=dim,
        )
    return cells


def layer_norm(values, gain):
    centre = values - jnp.mean(values, -1, keepdims=True)
    spread = jnp.mean(centre * centre, -1, keepdims=True)
    return centre * lax.rsqrt(spread + EPSILON) * gain


def rotary_tables(positions):
    half = HEAD_DIM // 2
    freqs = jnp.exp(jnp.arange(half, dtype=jnp.float32) * (-2.0 * math.log(10000.0) / HEAD_DIM))
    angles = positions.astype(jnp.float32)[:, None] * freqs[None, :]
    angles = jnp.concatenate([angles, angles], -1)[:, None, :]
    return (jnp.cos(angles), jnp.sin(angles))


def rotate(values, cosine, sine):
    half = values.shape[-1] // 2
    turned = jnp.concatenate([-values[..., half:], values[..., :half]], -1)
    return values * cosine + turned * sine


def unrotate(grads, cosine, sine):
    pull = jax.vjp(lambda inner: rotate(inner, cosine, sine), grads)[1]
    return pull(grads)[0]


def gated(gate, up):
    return jax.nn.gelu(gate, approximate=False) * up


def window_mask(positions, rest, rows, place, count):
    query_rows = jnp.arange(rows, dtype=jnp.int32)[:, None]
    key_cols = jnp.arange(rows + 2 * WINDOW, dtype=jnp.int32)[None, :]
    offset = key_cols - WINDOW - query_rows
    allowed = (
        (jnp.abs(offset) <= WINDOW) & (-offset <= positions[:, None]) & (offset <= rest[:, None])
    )
    allowed = allowed & ((key_cols >= WINDOW) | (place > 0))
    allowed = allowed & ((key_cols < rows + WINDOW) | (place < count - 1))
    return allowed


def on_device(
    tokens,
    cotangent,
    positions,
    rest,
    first_gain,
    second_gain,
    merged_weight,
    output_weight,
    input_weight,
    down_weight,
):
    gathered = (
        lax.all_gather(first_gain, "shard", axis=0, tiled=True),
        lax.all_gather(second_gain, "shard", axis=0, tiled=True),
        lax.all_gather(merged_weight, "shard", axis=0, tiled=True),
        lax.all_gather(output_weight, "shard", axis=0, tiled=True),
        lax.all_gather(input_weight, "shard", axis=0, tiled=True),
        lax.all_gather(down_weight, "shard", axis=0, tiled=True),
    )
    gain_one, gain_two, merged_full, output_full, input_full, down_full = gathered
    rows = tokens.shape[0]
    place = lax.axis_index(("replica", "shard"))
    count = lax.axis_size(("replica", "shard"))
    scale = HEAD_DIM ** (-0.5)
    tokens_f = tokens.astype(jnp.float32)
    norm_one, pull_one = jax.vjp(layer_norm, tokens_f, gain_one.astype(jnp.float32))
    norm_one_low = norm_one.astype(jnp.bfloat16)
    merged = jnp.dot(norm_one_low, merged_full, preferred_element_type=jnp.float32)
    cosine, sine = rotary_tables(positions)
    query = rotate(merged[:, :D].reshape(rows, HEADS, HEAD_DIM), cosine, sine).astype(jnp.bfloat16)
    keys = rotate(merged[:, D : 2 * D].reshape(rows, HEADS, HEAD_DIM), cosine, sine).astype(
        jnp.bfloat16
    )
    values = merged[:, 2 * D :].astype(jnp.bfloat16)
    pairs = jnp.concatenate([keys.reshape(rows, D), values], 1)
    pairs_wide = extended(pairs, ((("replica", "shard"), 0),), WINDOW)
    keys_wide = pairs_wide[:, :D].reshape(-1, HEADS, HEAD_DIM)
    values_wide = pairs_wide[:, D:].reshape(-1, HEADS, HEAD_DIM)
    allowed = window_mask(positions, rest, rows, place, count)[None]
    scores = (
        jnp.einsum("qhd,khd->hqk", query, keys_wide, preferred_element_type=jnp.float32) * scale
    )
    scores = jnp.where(allowed, scores, NEGATIVE)
    peak = jnp.max(scores, -1, keepdims=True)
    expo = jnp.exp(scores - peak)
    total = jnp.sum(expo, -1, keepdims=True)
    log_total = peak + jnp.log(total)
    prob = expo / total
    context = jnp.einsum(
        "hqk,khd->qhd", prob.astype(jnp.bfloat16), values_wide, preferred_element_type=jnp.float32
    )
    context = context.reshape(rows, D).astype(jnp.bfloat16)
    resid = tokens_f + jnp.dot(context, output_full, preferred_element_type=jnp.float32)
    norm_two, pull_two = jax.vjp(layer_norm, resid, gain_two.astype(jnp.float32))
    norm_two_low = norm_two.astype(jnp.bfloat16)
    hidden = jnp.dot(norm_two_low, input_full, preferred_element_type=jnp.float32)
    act, pull_act = jax.vjp(gated, hidden[:, :FF], hidden[:, FF:])
    act_low = act.astype(jnp.bfloat16)
    mixed = (resid + jnp.dot(act_low, down_full, preferred_element_type=jnp.float32)).astype(
        jnp.bfloat16
    )
    merged_back, output_back, input_back, down_back = (
        lax.all_gather(merged_weight, "shard", axis=0, tiled=True),
        lax.all_gather(output_weight, "shard", axis=0, tiled=True),
        lax.all_gather(input_weight, "shard", axis=0, tiled=True),
        lax.all_gather(down_weight, "shard", axis=0, tiled=True),
    )
    down_grad = jnp.einsum("tf,td->fd", act_low, cotangent, preferred_element_type=jnp.float32)
    grad_act = jnp.einsum("td,fd->tf", cotangent, down_back, preferred_element_type=jnp.float32)
    grad_gate, grad_up = pull_act(grad_act)
    grad_hidden = jnp.concatenate([grad_gate, grad_up], 1).astype(jnp.bfloat16)
    input_grad = jnp.einsum(
        "td,tf->df", norm_two_low, grad_hidden, preferred_element_type=jnp.float32
    )
    grad_norm_two = jnp.einsum(
        "tf,df->td", grad_hidden, input_back, preferred_element_type=jnp.float32
    )
    grad_resid_norm, second_gain_grad = pull_two(grad_norm_two)
    grad_resid = cotangent.astype(jnp.float32) + grad_resid_norm
    grad_resid_low = grad_resid.astype(jnp.bfloat16)
    output_grad = jnp.einsum(
        "td,te->de", context, grad_resid_low, preferred_element_type=jnp.float32
    )
    grad_context = jnp.einsum(
        "te,de->td", grad_resid_low, output_back, preferred_element_type=jnp.float32
    )
    grad_context = grad_context.astype(jnp.bfloat16).reshape(rows, HEADS, HEAD_DIM)
    scores_again = (
        jnp.einsum("qhd,khd->hqk", query, keys_wide, preferred_element_type=jnp.float32) * scale
    )
    scores_again = jnp.where(allowed, scores_again, NEGATIVE)
    prob_again = jnp.exp(scores_again - log_total)
    value_grad = jnp.einsum(
        "hqk,qhd->khd",
        prob_again.astype(jnp.bfloat16),
        grad_context,
        preferred_element_type=jnp.float32,
    )
    grad_prob = jnp.einsum(
        "qhd,khd->hqk", grad_context, values_wide, preferred_element_type=jnp.float32
    )
    grad_scores = prob_again * (grad_prob - jnp.sum(prob_again * grad_prob, -1, keepdims=True))
    grad_scores = grad_scores.astype(jnp.bfloat16)
    query_grad = (
        jnp.einsum("hqk,khd->qhd", grad_scores, keys_wide, preferred_element_type=jnp.float32)
        * scale
    )
    key_grad = (
        jnp.einsum("hqk,qhd->khd", grad_scores, query, preferred_element_type=jnp.float32) * scale
    )
    pair_grads = jnp.concatenate([key_grad.reshape(-1, D), value_grad.reshape(-1, D)], 1)
    middle = jnp.zeros((rows - 2 * WINDOW, 2 * D), jnp.float32)
    rims = jnp.concatenate([pair_grads[:WINDOW], middle, pair_grads[rows + WINDOW :]], 0)
    arrived = extended(rims.astype(jnp.bfloat16), ((("replica", "shard"), 0),), WINDOW).astype(
        rims.dtype
    )
    pair_own = pair_grads[WINDOW : rows + WINDOW] + jnp.concatenate(
        [arrived[:WINDOW], middle, arrived[rows + WINDOW :]], 0
    )
    grad_merged = jnp.concatenate(
        [
            unrotate(query_grad, cosine, sine).reshape(rows, D),
            unrotate(pair_own[:, :D].reshape(rows, HEADS, HEAD_DIM), cosine, sine).reshape(rows, D),
            pair_own[:, D:],
        ],
        1,
    ).astype(jnp.bfloat16)
    merged_grad = jnp.einsum(
        "td,te->de", norm_one_low, grad_merged, preferred_element_type=jnp.float32
    )
    grad_norm_one = jnp.einsum(
        "te,de->td", grad_merged, merged_back, preferred_element_type=jnp.float32
    )
    grad_tokens_norm, first_gain_grad = pull_one(grad_norm_one)
    token_grad = grad_resid + grad_tokens_norm
    shares = (
        lax.psum_scatter(
            first_gain_grad.astype(jnp.bfloat16), "shard", scatter_dimension=0, tiled=True
        ).astype(jnp.float32),
        lax.psum_scatter(
            second_gain_grad.astype(jnp.bfloat16), "shard", scatter_dimension=0, tiled=True
        ).astype(jnp.float32),
        lax.psum_scatter(
            merged_grad.astype(jnp.bfloat16), "shard", scatter_dimension=0, tiled=True
        ).astype(jnp.float32),
        lax.psum_scatter(
            output_grad.astype(jnp.bfloat16), "shard", scatter_dimension=0, tiled=True
        ).astype(jnp.float32),
        lax.psum_scatter(
            input_grad.astype(jnp.bfloat16), "shard", scatter_dimension=0, tiled=True
        ).astype(jnp.float32),
        lax.psum_scatter(
            down_grad.astype(jnp.bfloat16), "shard", scatter_dimension=0, tiled=True
        ).astype(jnp.float32),
    )
    summed = (
        lax.psum(shares[0].astype(jnp.bfloat16), "replica").astype(jnp.float32),
        lax.psum(shares[1].astype(jnp.bfloat16), "replica").astype(jnp.float32),
        lax.psum(shares[2].astype(jnp.bfloat16), "replica").astype(jnp.float32),
        lax.psum(shares[3].astype(jnp.bfloat16), "replica").astype(jnp.float32),
        lax.psum(shares[4].astype(jnp.bfloat16), "replica").astype(jnp.float32),
        lax.psum(shares[5].astype(jnp.bfloat16), "replica").astype(jnp.float32),
    )
    return (mixed, token_grad, summed[0], summed[1], summed[2], summed[3], summed[4], summed[5])


def solution(mesh):
    return jax.shard_map(
        on_device,
        mesh=mesh,
        in_specs=(
            P(("replica", "shard"), None),
            P(("replica", "shard"), None),
            P(("replica", "shard")),
            P(("replica", "shard")),
            P("shard"),
            P("shard"),
            P("shard", None),
            P("shard", None),
            P("shard", None),
            P("shard", None),
        ),
        out_specs=(
            P(("replica", "shard"), None),
            P(("replica", "shard"), None),
            P("shard"),
            P("shard"),
            P("shard", None),
            P("shard", None),
            P("shard", None),
            P("shard", None),
        ),
        check_vma=False,
    )
```

profile of v0, /device:TPU:0, one launch (start us, length us, event | category | flops | bytes accessed | tf_op | source)
XLA Modules:
  0.0 490.1 jit_solution(6088580094437044725)
XLA Ops:
  10.1 5.2 %all-gather = bf16[2,1,384]{2,1,0:T(2,128)(2,1)S(1)} all-gather(bf16[1,1,384]{2,1,0:T(2,128)(2,1)S(1)} %reshape.288), channel_id=1, replica_groups=mesh['replica'=16,'shard'=2] {'shard'}, dimensions={0}, use_global_device_ids=true | all-gather | bytes 2304 | tf_op jit(solution)/shard_map/all_gather | solution.py:90
  15.9 0.8 broadcast_multiply_fusion.3
  17.4 1.1 copy.38
  18.6 4.3 all-gather.1
  22.9 0.9 fusion.37
  23.8 37.8 %all-gather.7.cloned.1.call-done = bf16[768,2304]{1,0:T(8,128)(2,1)} async-done(((bf16[384,2304]{1,0:T(8,128)(2,1)}), bf16[768,2304]{1,0:T(8,128)(2,1)}) %all-gather.7.cloned.1.call-update) | async-done | bytes 3538960 | tf_op jit(solution)/shard_map/all_gather | solution.py:92
  61.6 3.1 fusion.49
  64.8 0.9 slice.86
  65.8 2.3 copy.39
  68.1 1.3 slice_negate_fusion.3
  69.3 0.9 maximum_multiply_fusion
  70.3 2.3 copy.40
  72.6 2.4 fusion.55
  75.0 1.4 collective-permute-start.1
  76.4 4.7 collective-permute-start
  82.5 6.5 %collective-permute-done.1 = bf16[64,1536]{1,0:T(8,128)(2,1)S(1)} collective-permute-done((bf16[64,1536]{1,0:T(8,128)(2,1)S(1)}, bf16[64,1536]{1,0:T(8,128)(2,1)S(1)}, u32[]{:S(2)}, u32[]{:S(2)}) %collective-permute-start.1) | collective-permute-done | bytes 196640 | tf_op jit(solution)/shard_map/ppermute | solution.py:29
  89.0 1.6 collective-permute-done
  91.7 1.0 fusion.61
  92.7 1.3 fusion
  94.1 0.8 copy-done
  94.9 1.7 fusion.10
  96.6 2.0 fusion.62
  99.4 44.6 %all-gather.11.cloned.1.call-done = bf16[768,2304]{1,0:T(8,128)(2,1)} async-done(((bf16[384,2304]{1,0:T(8,128)(2,1)}), bf16[768,2304]{1,0:T(8,128)(2,1)}) %all-gather.11.cloned.1.call-update) | async-done | bytes 3538960 | tf_op jit(solution)/shard_map/all_gather | solution.py:94
  144.1 3.2 fusion.52
  147.2 27.7 %all-gather.13.cloned.1.call-done = bf16[1152,768]{1,0:T(8,128)(2,1)} async-done(((bf16[576,768]{1,0:T(8,128)(2,1)}), bf16[1152,768]{1,0:T(8,128)(2,1)}) %all-gather.13.cloned.1.call-update) | async-done | bytes 1769488 | tf_op jit(solution)/shard_map/all_gather | solution.py:95
  174.9 4.7 add_convert_fusion
  179.6 1.1 multiply_convert_fusion.1
  180.8 1.5 copy-done.12
  182.3 1.8 multiply_reduce_fusion.1
  184.5 0.8 copy-done.2
  185.7 1.5 convolution_convert_fusion.3
  187.3 1.9 convolution_convert_fusion.2
  189.3 1.0 copy-done.20
  190.5 3.0 convolution_convert_fusion
  193.9 0.9 copy-done.8
  194.8 1.3 convolution_convert_fusion.4
  196.0 1.2 copy.44
  197.3 3.7 multiply_reduce_fusion
  201.2 1.1 multiply_convert_fusion
  203.3 1.3 fusion.3
  205.0 2.3 collective-permute-start.2
  207.3 1.3 collective-permute-start.3
  208.6 1.8 broadcast_multiply_fusion
  210.3 1.0 fusion.59
  211.3 11.7 %collective-permute-done.2 = bf16[64,1536]{0,1:T(8,128)(2,1)S(1)} collective-permute-done((bf16[64,1536]{0,1:T(8,128)(2,1)S(1)}, bf16[64,1536]{0,1:T(8,128)(2,1)S(1)}, u32[]{:S(2)}, u32[]{:S(2)}) %collective-permute-start.2) | collective-permute-done | bytes 196640 | tf_op jit(solution)/shard_map/ppermute | solution.py:27
  223.0 9.0 %collective-permute-done.3 = bf16[64,1536]{0,1:T(8,128)(2,1)S(1)} collective-permute-done((bf16[64,1536]{0,1:T(8,128)(2,1)S(1)}, bf16[64,1536]{0,1:T(8,128)(2,1)S(1)}, u32[]{:S(2)}, u32[]{:S(2)}) %collective-permute-start.3) | collective-permute-done | bytes 196640 | tf_op jit(solution)/shard_map/ppermute | solution.py:29
  232.8 0.8 broadcast_in_dim.54
  233.6 3.8 concatenate.50
  237.3 1.3 fusion.56
  243.0 3.1 convolution_convert_fusion.1
  246.2 1.0 reduce-scatter.11.cloned.1.call-done
  247.2 50.6 %reduce-scatter.9.cloned.1.call-done = bf16[384,2304]{1,0:T(8,128)(2,1)} async-done(((bf16[768,2304]{1,0:T(8,128)(2,1)}), bf16[384,2304]{1,0:T(8,128)(2,1)}) %reduce-scatter.9.cloned.1.call-update) | async-done | bytes 1769488 | tf_op jit(solution)/shard_map/reduce_scatter | solution.py:226
  297.8 50.6 %reduce-scatter.5.cloned.1.call-done = bf16[384,2304]{1,0:T(8,128)(2,1)} async-done(((bf16[768,2304]{1,0:T(8,128)(2,1)}), bf16[384,2304]{1,0:T(8,128)(2,1)}) %reduce-scatter.5.cloned.1.call-update) | async-done | bytes 1769488 | tf_op jit(solution)/shard_map/reduce_scatter | solution.py:220
  350.3 1.4 fusion.9
  352.4 2.5 fusion.27
  355.6 4.9 %all-reduce.8 = (bf16[768]{0:T(1024)(128)(2,1)S(1)}, bf16[768]{0:T(1024)(128)(2,1)S(1)}) all-reduce(bf16[768]{0:T(1024)(128)(2,1)S(1)} %get-tuple-element.10, bf16[768]{0:T(1024)(128)(2,1)S(1)} %copy-done.64), channel_id=2, replica_groups=mesh['replica'=16,'shard'=2] {'shard'}, use_global_device_ids=true, to_apply=%region_12.13.clone | all-reduce | flops 1536 | bytes 6144
  360.7 33.7 %all-reduce.6 = (bf16[384]{0:T(512)(128)(2,1)S(1)}, bf16[384]{0:T(512)(128)(2,1)S(1)}) all-reduce(bf16[384]{0:T(512)(128)(2,1)S(1)} %dynamic-slice.1, bf16[384]{0:T(512)(128)(2,1)S(1)} %dynamic-slice.3), channel_id=1, replica_groups=mesh['replica'=16,'shard'=2] {'replica'}, use_global_device_ids=true, to_apply=%region_13.14 | all-reduce | flops 768 | bytes 3072 | tf_op jit(solution)/shard_map/psum | solution.py:234
  395.6 1.3 add_add_fusion.2
  396.8 77.9 %all-reduce.11.cloned.1.call-done = (bf16[384,2304]{1,0:T(8,128)(2,1)}, bf16[384,768]{1,0:T(8,128)(2,1)}, bf16[384,2304]{1,0:T(8,128)(2,1)}, bf16[576,768]{1,0:T(8,128)(2,1)}) async-done(((bf16[384,2304]{1,0:T(8,128)(2,1)}, bf16[384,768]{1,0:T(8,128)(2,1)}, bf16[384,2304]{1,0:T(8,128)(2,1)}, bf16[576,768]{1,0:T(8,128)(2,1)}), (bf16[384,2304]{1,0:T(8,128)(2,1)}, bf16[384,768]{1,0:T(8,128)(2,1)}, ...) | async-done | bytes 5013520 | tf_op jit(solution)/shard_map/psum | solution.py:236
  474.8 3.6 convert_element_type.138
  478.3 1.1 convert_element_type.140
  479.4 0.8 copy-done.24
  480.2 2.0 convert_element_type.142
  482.3 1.3 convert_element_type.144
  (210 shorter events, 19.2 us)
Async XLA Ops:
  7.2 54.5 %all-gather.7.cloned.1.call-start = ((), (), s32[]{:S(2)}) async-start(), calls=%async_computation.4 | async-start | bytes 5308416 | tf_op jit(solution)/shard_map/all_gather | solution.py:92
  7.9 88.7 %all-gather.9.cloned.1.call-start = ((), (), s32[]{:S(2)}) async-start(), calls=%async_computation.5 | async-start | bytes 1769472 | tf_op jit(solution)/shard_map/all_gather | solution.py:93
  8.7 1.4 copy-start.66
  8.7 6.7 %copy-start.1 = (bf16[256,768]{1,0:T(8,128)(2,1)S(1)}, bf16[256,768]{1,0:T(8,128)(2,1)}, u32[]{:S(2)}) copy-start(bf16[256,768]{1,0:T(8,128)(2,1)} %param.10) | copy-start | bytes 1179652
  8.7 135.4 %all-gather.11.cloned.1.call-start = ((), (), s32[]{:S(2)}) async-start(), calls=%async_computation.6 | async-start | bytes 5308416 | tf_op jit(solution)/shard_map/all_gather | solution.py:94
  9.4 6.4 %copy-start.63 = (s32[256]{0:T(256)S(1)}, s32[256]{0:T(256)}, u32[]{:S(2)}) copy-start(s32[256]{0:T(256)} %param.12) | copy-start | bytes 3076
  9.4 165.5 %all-gather.13.cloned.1.call-start = ((), (), s32[]{:S(2)}) async-start(), calls=%async_computation.7 | async-start | bytes 2654208 | tf_op jit(solution)/shard_map/all_gather | solution.py:95
  10.0 236.2 %reduce-scatter.7.cloned.1.call-start = ((), (), s32[]{:S(2)}) async-start(), calls=%async_computation.9 | async-start | bytes 1769472 | tf_op jit(solution)/shard_map/reduce_scatter | solution.py:223
  15.8 45.9 %copy-start.55 = (f32[256]{0:T(256)}, f32[256]{0:T(256)S(1)}, u32[]{:S(2)}) copy-start(f32[256]{0:T(256)S(1)} %fusion.42) | copy-start | bytes 3076
  17.3 1.2 copy-start.67
  17.3 5.6 %copy-start.65 = (s32[256]{0:T(256)S(1)}, s32[256]{0:T(256)}, u32[]{:S(2)}) copy-start(s32[256]{0:T(256)} %param.13) | copy-start | bytes 3076
  68.1 1.3 copy-start.34
  75.0 6.2 %copy-start.18 = (f32[256,768]{1,0:T(8,128)S(1)}, f32[256,768]{1,0:T(8,128)}, u32[]{:S(2)}) copy-start(f32[256,768]{1,0:T(8,128)} %get-tuple-element.26) | copy-start | bytes 2359300
  75.0 14.0 %collective-permute-start.1 = (bf16[64,1536]{1,0:T(8,128)(2,1)S(1)}, bf16[64,1536]{1,0:T(8,128)(2,1)S(1)}, u32[]{:S(2)}, u32[]{:S(2)}) collective-permute-start(bf16[64,1536]{1,0:T(8,128)(2,1)S(1)} %get-tuple-element.41), channel_id=1, source_target_pairs={{1,0},{2,1},{3,2},{4,3},{5,4},{6,5},{7,6},{8,7},{9,8},{10,9},{11,1... | collective-permute-start | bytes 589832 | tf_op jit(solution)/shard_map/ppermute | solution.py:29
  76.4 14.2 %collective-permute-start = (bf16[64,1536]{1,0:T(8,128)(2,1)S(1)}, bf16[64,1536]{1,0:T(8,128)(2,1)S(1)}, u32[]{:S(2)}, u32[]{:S(2)}) collective-permute-start(bf16[64,1536]{1,0:T(8,128)(2,1)S(1)} %get-tuple-element.40), channel_id=1, source_target_pairs={{0,1},{1,2},{2,3},{3,4},{4,5},{5,6},{6,7},{7,8},{8,9},{9,10},{10,1... | collective-permute-start | bytes 589832 | tf_op jit(solution)/shard_map/ppermute | solution.py:27
  82.5 8.9 %copy-start.13 = (bf16[256,12,64]{0,2,1:T(8,128)(2,1)}, bf16[256,12,64]{0,2,1:T(8,128)(2,1)S(1)}, u32[]{:S(2)}) copy-start(bf16[256,12,64]{0,2,1:T(8,128)(2,1)S(1)} %fusion.29) | copy-start | bytes 1179652
  91.1 3.0 copy-start.21
  91.4 1.3 copy-start.6
  92.7 2.2 copy-start
  92.7 2.2 copy-start.49
  94.0 2.5 copy-start.51
  96.6 2.0 copy-start.27
  179.6 2.6 copy-start.12
  179.6 2.6 copy-start.53
  180.8 3.3 copy-start.19
  182.3 1.8 copy-start.60
  184.1 1.2 copy-start.15
  184.4 1.3 copy-start.28
  184.4 2.8 copy-start.61
  185.7 1.6 copy-start.4
  187.3 59.9 %reduce-scatter.11.cloned.1.call-start = ((), (), s32[]{:S(2)}) async-start(), calls=%async_computation.11 | async-start | bytes 2654208 | tf_op jit(solution)/shard_map/reduce_scatter | solution.py:229
  189.2 1.2 copy-start.39
  189.2 1.2 copy-start.54
  189.2 108.5 %reduce-scatter.9.cloned.1.call-start = ((), (), s32[]{:S(2)}) async-start(), calls=%async_computation.10 | async-start | bytes 5308416 | tf_op jit(solution)/shard_map/reduce_scatter | solution.py:226
  193.5 1.3 copy-start.8
  193.5 154.9 %reduce-scatter.5.cloned.1.call-start = ((), (), s32[]{:S(2)}) async-start(), calls=%async_computation.8 | async-start | bytes 5308416 | tf_op jit(solution)/shard_map/reduce_scatter | solution.py:220
  194.8 2.4 copy-start.50
  194.8 2.4 copy-start.52
  194.8 2.5 copy-start.22
  197.2 3.8 copy-start.9
  197.3 3.8 slice-start
  197.3 3.9 slice-start.1
  204.8 3.8 copy-start.7
  204.8 3.8 copy-start.48
  205.0 5.4 %copy-start.25 = (bf16[64,1536]{0,1:T(8,128)(2,1)}, bf16[64,1536]{0,1:T(8,128)(2,1)S(1)}, u32[]{:S(2)}) copy-start(bf16[64,1536]{0,1:T(8,128)(2,1)S(1)} %get-tuple-element.30) | copy-start | bytes 589828
  205.0 5.4 %copy-start.26 = (bf16[64,1536]{0,1:T(8,128)(2,1)}, bf16[64,1536]{0,1:T(8,128)(2,1)S(1)}, u32[]{:S(2)}) copy-start(bf16[64,1536]{0,1:T(8,128)(2,1)S(1)} %get-tuple-element.31) | copy-start | bytes 589828
  205.0 18.0 %collective-permute-start.2 = (bf16[64,1536]{0,1:T(8,128)(2,1)S(1)}, bf16[64,1536]{0,1:T(8,128)(2,1)S(1)}, u32[]{:S(2)}, u32[]{:S(2)}) collective-permute-start(bf16[64,1536]{0,1:T(8,128)(2,1)S(1)} %get-tuple-element.31), channel_id=1, source_target_pairs={{0,1},{1,2},{2,3},{3,4},{4,5},{5,6},{6,7},{7,8},{8,9},{9,10},{10,1... | collective-permute-start | bytes 589832 | tf_op jit(solution)/shard_map/ppermute | solution.py:27
  207.3 24.8 %collective-permute-start.3 = (bf16[64,1536]{0,1:T(8,128)(2,1)S(1)}, bf16[64,1536]{0,1:T(8,128)(2,1)S(1)}, u32[]{:S(2)}, u32[]{:S(2)}) collective-permute-start(bf16[64,1536]{0,1:T(8,128)(2,1)S(1)} %get-tuple-element.30), channel_id=1, source_target_pairs={{1,0},{2,1},{3,2},{4,3},{5,4},{6,5},{7,6},{8,7},{9,8},{10,9},{11,1... | collective-permute-start | bytes 589832 | tf_op jit(solution)/shard_map/ppermute | solution.py:29
  223.0 9.0 %copy-start.41 = (bf16[64,1536]{0,1:T(8,128)(2,1)}, bf16[64,1536]{0,1:T(8,128)(2,1)S(1)}, u32[]{:S(2)}) copy-start(bf16[64,1536]{0,1:T(8,128)(2,1)S(1)} %collective-permute-done.2) | copy-start | bytes 589828
  239.5 2.6 copy-start.43
  240.3 1.2 copy-start.29
  240.3 1.3 copy-start.30
  241.7 1.3 copy-start.56
  246.1 228.7 %all-reduce.11.cloned.1.call-start = ((), (), s32[]{:S(2)}) async-start(), calls=%async_computation.12 | async-start | bytes 10027008 | tf_op jit(solution)/shard_map/psum | solution.py:236
  348.4 1.9 copy-start.5
  348.4 1.9 copy-start.23
  350.3 2.1 copy-start.11
  352.4 2.5 copy-start.58
  354.9 40.7 %copy-start.3 = (f32[256,768]{1,0:T(8,128)S(1)}, f32[256,768]{1,0:T(8,128)}, u32[]{:S(2)}) copy-start(f32[256,768]{1,0:T(8,128)} %copy-done.2) | copy-start | bytes 2359300
  354.9 40.6 %copy-start.16 = (bf16[256,768]{1,0:T(8,128)(2,1)S(1)}, bf16[256,768]{1,0:T(8,128)(2,1)}, u32[]{:S(2)}) copy-start(bf16[256,768]{1,0:T(8,128)(2,1)} %param.11) | copy-start | bytes 1179652
  354.9 40.6 %copy-start.62 = (f32[256]{0:T(256)S(1)}, f32[256]{0:T(256)}, u32[]{:S(2)}) copy-start(f32[256]{0:T(256)} %copy-done.61) | copy-start | bytes 3076
  474.8 3.6 copy-start.40
  478.3 1.9 copy-start.24
  480.2 2.0 copy-start.37
  (20 other events, 17.4 us)
Sparse Core Ops, SparseCore 0:
  9.5 52.0 all-gather.6
  63.2 28.9 all-gather.8
  93.7 50.2 all-gather.10
  145.5 29.4 all-gather.12
  187.4 21.7 reduce-scatter.6
  212.0 35.1 reduce-scatter.10
  250.0 47.7 reduce-scatter.8
  300.7 47.6 reduce-scatter.4
  352.4 122.3 all-reduce.10
where the time goes:
time: 491 us; the launch traced here: 490 us
  waiting for transfers between devices  322 us (66%)
  blocking collectives  48.2 us (10%)
  matrix products  39.4 us (8%)
  local copies, waits for them, and re-layouts  29.8 us (6%)
  other arithmetic  25.2 us (5%)
  between operations  15.4 us (3%)
  starting transfers between devices  10.3 us (2%)
    psum x1, waiting for transfers between devices, on_device(): lax.psum(shares[2].astype(jnp.bfloat16), 'replica').astype(jnp.float32)  77.9 us
    reduce_scatter x1, waiting for transfers between devices, on_device(): lax.psum_scatter(input_grad.astype(jnp.bfloat16), 'shard', scatter_dimens...  50.6 us
    reduce_scatter x1, waiting for transfers between devices, on_device(): lax.psum_scatter(merged_grad.astype(jnp.bfloat16), 'shard', scatter_dimen...  50.6 us
    all_gather x1, waiting for transfers between devices, on_device(): lax.all_gather(input_weight, 'shard', axis=0, tiled=True)  44.6 us
    all_gather x1, waiting for transfers between devices, on_device(): lax.all_gather(merged_weight, 'shard', axis=0, tiled=True)  37.8 us
    psum x1, blocking collectives, on_device(): lax.psum(shares[0].astype(jnp.bfloat16), 'replica').astype(jnp.float32)  33.7 us
    all_gather x1, waiting for transfers between devices, on_device(): lax.all_gather(down_weight, 'shard', axis=0, tiled=True)  27.7 us
    ppermute x2, waiting for transfers between devices, extended(): lax.ppermute(head, axis, [((i + 1) % count, i) for i in range(ends)])  15.5 us
  transfers between devices with their start and end apart: 13, of which 11 were waited for; matrix products, arithmetic and copies ran while one was open for 13% of the time, Pallas kernels for 0%

commit v1 on v0

--- a/solution.py
+++ b/solution.py
@@ -1,8 +1,11 @@
+import functools
 import math
 
 import jax
 import jax.numpy as jnp
 from jax import lax
+from jax.experimental import pallas as pl
+from jax.experimental.pallas import tpu as pltpu
 from jax.sharding import PartitionSpec as P
 
 D = 768
@@ -74,6 +77,354 @@
     return allowed
 
 
+PACK = 768
+UNIT = 16
+MESH = pl.DeviceIdType.MESH
+
+
+def greet(peers):
+    barrier = pltpu.get_barrier_semaphore()
+    for peer in peers:
+        pl.semaphore_signal(barrier, inc=1, device_id=peer, device_id_type=MESH)
+    pl.semaphore_wait(barrier, len(peers))
+
+
+def gather_kernel(shards, splits, *refs):
+    count = len(splits)
+    sources, fulls = refs[:count], refs[count : 2 * count]
+    send_sem, recv_sem = refs[2 * count :]
+    replica = lax.axis_index("replica")
+    me = lax.axis_index("shard")
+    core = lax.rem(replica, 2)
+    side = lax.rem(lax.div(replica, 2), 2)
+    core_peer = (replica + 1 - 2 * core, me)
+    side_peer = (replica + 2 - 4 * side, me)
+    greet(
+        [(replica, lax.rem(me + off, shards)) for off in range(1, shards)] + [core_peer, side_peer]
+    )
+
+    def part(which, row_half, col_half):
+        rows, cols = sources[which].shape
+        by_rows, by_cols = splits[which]
+        take_rows, take_cols = pl.ds(0, rows), pl.ds(0, cols)
+        if by_rows:
+            take_rows = pl.ds(pl.multiple_of(row_half * (rows // 2), UNIT), rows // 2)
+        if by_cols:
+            take_cols = pl.ds(pl.multiple_of(col_half * (cols // 2), 128), cols // 2)
+        return take_rows, take_cols
+
+    def copy(which, off, kind, source, target, peer):
+        return pltpu.make_async_remote_copy(
+            src_ref=source,
+            dst_ref=target,
+            send_sem=send_sem.at[which, off - 1, kind],
+            recv_sem=recv_sem.at[which, off - 1, kind],
+            device_id=peer,
+            device_id_type=MESH,
+        )
+
+    def place(which, owner, row_half, col_half):
+        return fulls[which].at[(owner,) + part(which, row_half, col_half)]
+
+    copies = {}
+    for which in range(count):
+        for off in range(1, shards):
+            copies[which, off, 0] = copy(
+                which,
+                off,
+                0,
+                sources[which].at[part(which, side, core)],
+                place(which, me, side, core),
+                (replica, lax.rem(me + off, shards)),
+            )
+            copies[which, off, 0].start()
+    for which in range(count):
+        fulls[which][me] = sources[which][...]
+
+    def forward(which):
+        by_rows, by_cols = splits[which]
+        for off in range(1, shards):
+            owner = lax.rem(me + shards - off, shards)
+            piece = place(which, owner, side, core)
+            copies[which, off, 0].wait_recv()
+            if by_rows:
+                copies[which, off, 1] = copy(which, off, 1, piece, piece, side_peer)
+                copies[which, off, 1].start()
+            if by_cols:
+                copies[which, off, 2] = copy(which, off, 2, piece, piece, core_peer)
+                copies[which, off, 2].start()
+
+    def cross(which):
+        by_rows, by_cols = splits[which]
+        for off in range(1, shards):
+            owner = lax.rem(me + shards - off, shards)
+            if by_rows:
+                copies[which, off, 1].wait_recv()
+                if by_cols:
+                    piece = place(which, owner, 1 - side, core)
+                    copies[which, off, 3] = copy(which, off, 3, piece, piece, core_peer)
+                    copies[which, off, 3].start()
+
+    for which in range(count + 1):
+        if which < count:
+            forward(which)
+        if which > 0:
+            cross(which - 1)
+    for which in range(count):
+        for off in range(1, shards):
+            for kind in (2, 3):
+                if (which, off, kind) in copies:
+                    copies[which, off, kind].wait_recv()
+    for one in copies.values():
+        one.wait_send()
+
+
+def gather_weights(weights, shards):
+    splits = tuple(
+        (w.shape[0] % (2 * UNIT) == 0, w.shape[1] % 256 == 0 and w.shape[0] > UNIT)
+        for w in weights
+    )
+    count = len(weights)
+    fulls = pl.pallas_call(
+        functools.partial(gather_kernel, shards, splits),
+        out_shape=[jax.ShapeDtypeStruct((shards,) + w.shape, w.dtype) for w in weights],
+        in_specs=[pl.BlockSpec(memory_space=pltpu.VMEM)] * count,
+        out_specs=[pl.BlockSpec(memory_space=pltpu.VMEM)] * count,
+        scratch_shapes=[
+            pltpu.SemaphoreType.DMA((count, shards - 1, 4)),
+            pltpu.SemaphoreType.DMA((count, shards - 1, 4)),
+        ],
+        compiler_params=pltpu.CompilerParams(
+            collective_id=0, has_side_effects=True, vmem_limit_bytes=40 * 1024 * 1024
+        ),
+        name="gather_weights",
+    )(*weights)
+    return fulls
+
+
+def reduce_kernel(shards, depth, chunks, rows, count, *refs):
+    matrices, total = refs[:count], refs[count]
+    terms, core_in, shard_in, side_in, deep_in, packs, sends, recvs = refs[count + 1 :]
+    loads, filled = [], 0
+    for matrix in matrices:
+        taken = matrix.shape[1]
+        for left in range(0, matrix.shape[2], PACK):
+            load = pltpu.make_async_copy(
+                matrix.at[:, :, pl.ds(left, PACK)],
+                terms.at[:, pl.ds(filled, taken), :],
+                packs.at[len(loads)],
+            )
+            load.start()
+            loads.append(load)
+            filled += taken
+    if filled < chunks * rows:
+        terms[:, filled:, :] = jnp.zeros((shards, chunks * rows - filled, PACK), terms.dtype)
+    replica = lax.axis_index("replica")
+    me = lax.axis_index("shard")
+    core = lax.rem(replica, 2)
+    side = lax.rem(lax.div(replica, 2), 2)
+    level = lax.div(replica, 4)
+    half, quarter, leaf = rows // 2, rows // 4, rows // (4 * depth)
+    core_peer = (replica + 1 - 2 * core, me)
+    side_peer = (replica + 2 - 4 * side, me)
+    shard_peers = [(replica, lax.rem(me + off, shards)) for off in range(1, shards)]
+    levels = [lax.rem(level + off, depth) for off in range(1, depth)]
+    deep_peers = [(4 * other + lax.rem(replica, 4), me) for other in levels]
+    greet([core_peer, side_peer] + shard_peers + deep_peers)
+    for load in loads:
+        load.wait()
+    first_shard, first_side, first_deep = 1, shards, shards + 1
+    back_deep, back_side, back_core = shards + depth, shards + 2 * depth - 1, shards + 2 * depth
+
+    def copy(chunk, slot, source, target, peer):
+        return pltpu.make_async_remote_copy(
+            src_ref=source,
+            dst_ref=target,
+            send_sem=sends.at[chunk, slot],
+            recv_sem=recvs.at[chunk, slot],
+            device_id=peer,
+            device_id_type=MESH,
+        )
+
+    def span(start, size):
+        return pl.ds(pl.multiple_of(start, UNIT), size)
+
+    def wide(cells):
+        return cells.astype(jnp.float32)
+
+    def to_core(k):
+        source = terms.at[:, span(k * rows + (1 - core) * half, half), :]
+        return [copy(k, 0, source, core_in.at[k], core_peer)]
+
+    def to_shard(k):
+        return [
+            copy(
+                k,
+                first_shard + i,
+                core_in.at[k, lax.rem(me + i + 1, shards)],
+                shard_in.at[k, i],
+                shard_peers[i],
+            )
+            for i in range(shards - 1)
+        ]
+
+    def to_side(k):
+        source = core_in.at[k, me, span((1 - side) * quarter, quarter), :]
+        return [copy(k, first_side, source, side_in.at[k], side_peer)]
+
+    def to_deep(k):
+        return [
+            copy(
+                k,
+                first_deep + i,
+                side_in.at[k, span(levels[i] * leaf, leaf), :],
+                deep_in.at[k, i],
+                deep_peers[i],
+            )
+            for i in range(depth - 1)
+        ]
+
+    def same(k, slot, start, size, peer):
+        region = total.at[span(k * rows + start, size), :]
+        return copy(k, slot, region, region, peer)
+
+    def from_deep(k):
+        start = core * half + side * quarter + level * leaf
+        return [same(k, back_deep + i, start, leaf, deep_peers[i]) for i in range(depth - 1)]
+
+    def from_side(k):
+        return [same(k, back_side, core * half + side * quarter, quarter, side_peer)]
+
+    def from_core(k):
+        return [same(k, back_core, core * half, half, core_peer)]
+
+    def begin(copies):
+        for one in copies:
+            one.start()
+
+    def arrive(copies):
+        for one in copies:
+            one.wait_recv()
+
+    def step_start(k):
+        begin(to_core(k))
+
+    def step_core(k):
+        arrive(to_core(k))
+        own = terms[:, span(k * rows + core * half, half), :]
+        core_in[k] = (wide(own) + wide(core_in[k])).astype(core_in.dtype)
+        begin(to_shard(k))
+
+    def step_shard(k):
+        arrive(to_shard(k))
+        summed = wide(core_in[k, me])
+        for i in range(shards - 1):
+            summed = summed + wide(shard_in[k, i])
+        core_in[k, me] = summed.astype(core_in.dtype)
+        begin(to_side(k))
+
+    def step_side(k):
+        arrive(to_side(k))
+        own = core_in[k, me, span(side * quarter, quarter), :]
+        side_in[k] = (wide(own) + wide(side_in[k])).astype(side_in.dtype)
+        begin(to_deep(k))
+
+    def step_deep(k):
+        arrive(to_deep(k))
+        summed = wide(side_in[k, span(level * leaf, leaf), :])
+        for i in range(depth - 1):
+            summed = summed + wide(deep_in[k, i])
+        start = k * rows + core * half + side * quarter + level * leaf
+        total[span(start, leaf), :] = summed.astype(total.dtype)
+        begin(from_deep(k))
+
+    def step_back_deep(k):
+        arrive(from_deep(k))
+        begin(from_side(k))
+
+    def step_back_side(k):
+        arrive(from_side(k))
+        begin(from_core(k))
+
+    def step_back_core(k):
+        arrive(from_core(k))
+        for family in (to_core, to_shard, to_side, to_deep, from_deep, from_side, from_core):
+            for one in family(k):
+                one.wait_send()
+
+    steps = (
+        step_start,
+        step_core,
+        step_shard,
+        step_side,
+        step_deep,
+        step_back_deep,
+        step_back_side,
+        step_back_core,
+    )
+
+    def tick(t, carry):
+        for lag, step in enumerate(steps):
+            k = t - lag
+
+            @pl.when((k >= 0) & (k < chunks))
+            def _(step=step, k=k):
+                step(k)
+
+        return carry
+
+    lax.fori_loop(0, chunks + len(steps) - 1, tick, 0)
+
+
+def sum_grads(matrices, gains, shards, replicas, identity):
+    blocks = [
+        matrix.astype(jnp.bfloat16).reshape(shards, matrix.shape[0] // shards, -1)
+        for matrix in matrices
+    ]
+    if gains:
+        line = jnp.concatenate([g.astype(jnp.bfloat16).reshape(shards, 1, -1) for g in gains], 2)
+        blocks.append(jnp.pad(line, ((0, 0), (0, UNIT - 1), (0, PACK - line.shape[2]))))
+    pieces = [block.shape[1] for block in blocks for _ in range(0, block.shape[2], PACK)]
+    rows = UNIT * replicas
+    chunks = -(-sum(pieces) // rows)
+    depth = replicas // 4
+    slots = shards + 2 * depth + 1
+    kind = jnp.bfloat16
+    count = len(blocks)
+    total = pl.pallas_call(
+        functools.partial(reduce_kernel, shards, depth, chunks, rows, count),
+        out_shape=jax.ShapeDtypeStruct((chunks * rows, PACK), kind),
+        in_specs=[pl.BlockSpec(memory_space=pl.ANY)] * count,
+        out_specs=pl.BlockSpec(memory_space=pltpu.VMEM),
+        scratch_shapes=[
+            pltpu.VMEM((shards, chunks * rows, PACK), kind),
+            pltpu.VMEM((chunks, shards, rows // 2, PACK), kind),
+            pltpu.VMEM((chunks, shards - 1, rows // 2, PACK), kind),
+            pltpu.VMEM((chunks, rows // 4, PACK), kind),
+            pltpu.VMEM((chunks, depth - 1, UNIT, PACK), kind),
+            pltpu.SemaphoreType.DMA((len(pieces),)),
+            pltpu.SemaphoreType.DMA((chunks, slots)),
+            pltpu.SemaphoreType.DMA((chunks, slots)),
+        ],
+        compiler_params=pltpu.CompilerParams(
+            collective_id=identity, has_side_effects=True, vmem_limit_bytes=48 * 1024 * 1024
+        ),
+        name="reduce_terms",
+    )(*blocks)
+    results, start = [], 0
+    for matrix in matrices:
+        size = matrix.shape[0] // shards
+        parts = []
+        for _ in range(0, matrix.shape[1], PACK):
+            parts.append(total[start : start + size].astype(jnp.float32))
+            start += size
+        results.append(jnp.concatenate(parts, 1))
+    for i, gain in enumerate(gains):
+        size = gain.shape[0] // shards
+        results.append(total[start, i * size : (i + 1) * size].astype(jnp.float32))
+    return results
+
+
 def on_device(
     tokens,
     cotangent,
@@ -86,15 +437,19 @@
     input_weight,
     down_weight,
 ):
-    gathered = (
-        lax.all_gather(first_gain, "shard", axis=0, tiled=True),
-        lax.all_gather(second_gain, "shard", axis=0, tiled=True),
-        lax.all_gather(merged_weight, "shard", axis=0, tiled=True),
-        lax.all_gather(output_weight, "shard", axis=0, tiled=True),
-        lax.all_gather(input_weight, "shard", axis=0, tiled=True),
-        lax.all_gather(down_weight, "shard", axis=0, tiled=True),
-    )
-    gain_one, gain_two, merged_full, output_full, input_full, down_full = gathered
+    shards = lax.axis_size("shard")
+    replicas = lax.axis_size("replica")
+    gain_size = first_gain.shape[0]
+    gains = jnp.concatenate([first_gain, second_gain])[None, :]
+    gains = jnp.pad(gains, ((0, UNIT - 1), (0, -gains.shape[1] % 128)))
+    fulls = gather_weights(
+        [gains, merged_weight, output_weight, input_weight, down_weight], shards
+    )
+    gain_one = fulls[0][:, 0, :gain_size].reshape(-1)
+    gain_two = fulls[0][:, 0, gain_size : 2 * gain_size].reshape(-1)
+    merged_full, output_full, input_full, down_full = [
+        full.reshape(-1, full.shape[2]) for full in fulls[1:]
+    ]
     rows = tokens.shape[0]
     place = lax.axis_index(("replica", "shard"))
     count = lax.axis_size(("replica", "shard"))
@@ -136,21 +491,15 @@
     mixed = (resid + jnp.dot(act_low, down_full, preferred_element_type=jnp.float32)).astype(
         jnp.bfloat16
     )
-    merged_back, output_back, input_back, down_back = (
-        lax.all_gather(merged_weight, "shard", axis=0, tiled=True),
-        lax.all_gather(output_weight, "shard", axis=0, tiled=True),
-        lax.all_gather(input_weight, "shard", axis=0, tiled=True),
-        lax.all_gather(down_weight, "shard", axis=0, tiled=True),
-    )
     down_grad = jnp.einsum("tf,td->fd", act_low, cotangent, preferred_element_type=jnp.float32)
-    grad_act = jnp.einsum("td,fd->tf", cotangent, down_back, preferred_element_type=jnp.float32)
+    grad_act = jnp.einsum("td,fd->tf", cotangent, down_full, preferred_element_type=jnp.float32)
     grad_gate, grad_up = pull_act(grad_act)
     grad_hidden = jnp.concatenate([grad_gate, grad_up], 1).astype(jnp.bfloat16)
     input_grad = jnp.einsum(
         "td,tf->df", norm_two_low, grad_hidden, preferred_element_type=jnp.float32
     )
     grad_norm_two = jnp.einsum(
-        "tf,df->td", grad_hidden, input_back, preferred_element_type=jnp.float32
+        "tf,df->td", grad_hidden, input_full, preferred_element_type=jnp.float32
     )
     grad_resid_norm, second_gain_grad = pull_two(grad_norm_two)
     grad_resid = cotangent.astype(jnp.float32) + grad_resid_norm
@@ -159,7 +508,7 @@
         "td,te->de", context, grad_resid_low, preferred_element_type=jnp.float32
     )
     grad_context = jnp.einsum(
-        "te,de->td", grad_resid_low, output_back, preferred_element_type=jnp.float32
+        "te,de->td", grad_resid_low, output_full, preferred_element_type=jnp.float32
     )
     grad_context = grad_context.astype(jnp.bfloat16).reshape(rows, HEADS, HEAD_DIM)
     scores_again = (
@@ -206,39 +555,27 @@
         "td,te->de", norm_one_low, grad_merged, preferred_element_type=jnp.float32
     )
     grad_norm_one = jnp.einsum(
-        "te,de->td", grad_merged, merged_back, preferred_element_type=jnp.float32
+        "te,de->td", grad_merged, merged_full, preferred_element_type=jnp.float32
     )
     grad_tokens_norm, first_gain_grad = pull_one(grad_norm_one)
     token_grad = grad_resid + grad_tokens_norm
-    shares = (
-        lax.psum_scatter(
-            first_gain_grad.astype(jnp.bfloat16), "shard", scatter_dimension=0, tiled=True
-        ).astype(jnp.float32),
-        lax.psum_scatter(
-            second_gain_grad.astype(jnp.bfloat16), "shard", scatter_dimension=0, tiled=True
-        ).astype(jnp.float32),
-        lax.psum_scatter(
-            merged_grad.astype(jnp.bfloat16), "shard", scatter_dimension=0, tiled=True
-        ).astype(jnp.float32),
-        lax.psum_scatter(
-            output_grad.astype(jnp.bfloat16), "shard", scatter_dimension=0, tiled=True
-        ).astype(jnp.float32),
-        lax.psum_scatter(
-            input_grad.astype(jnp.bfloat16), "shard", scatter_dimension=0, tiled=True
-        ).astype(jnp.float32),
-        lax.psum_scatter(
-            down_grad.astype(jnp.bfloat16), "shard", scatter_dimension=0, tiled=True
-        ).astype(jnp.float32),
-    )
-    summed = (
-        lax.psum(shares[0].astype(jnp.bfloat16), "replica").astype(jnp.float32),
-        lax.psum(shares[1].astype(jnp.bfloat16), "replica").astype(jnp.float32),
-        lax.psum(shares[2].astype(jnp.bfloat16), "replica").astype(jnp.float32),
-        lax.psum(shares[3].astype(jnp.bfloat16), "replica").astype(jnp.float32),
-        lax.psum(shares[4].astype(jnp.bfloat16), "replica").astype(jnp.float32),
-        lax.psum(shares[5].astype(jnp.bfloat16), "replica").astype(jnp.float32),
-    )
-    return (mixed, token_grad, summed[0], summed[1], summed[2], summed[3], summed[4], summed[5])
+    merged_sum, output_sum, input_sum, down_sum, first_sum, second_sum = sum_grads(
+        [merged_grad, output_grad, input_grad, down_grad],
+        [first_gain_grad, second_gain_grad],
+        shards,
+        replicas,
+        1,
+    )
+    return (
+        mixed,
+        token_grad,
+        first_sum,
+        second_sum,
+        merged_sum,
+        output_sum,
+        input_sum,
+        down_sum,
+    )
 
 
 def solution(mesh):

time: 491 us -> 261 us (0.53)
  waiting for transfers between devices: 322 us -> 19.5 us
  Pallas kernels: 0 us -> 135 us
  blocking collectives: 48.2 us -> 0 us
  between operations: 15.4 us -> 1.46 us
  matrix products: 39.4 us -> 30 us
  local copies, waits for them, and re-layouts: 29.8 us -> 35.9 us
  other arithmetic: 25.2 us -> 31 us
    pallas_call x0 -> x2, Pallas kernels: none -> 135 us  [the longest x1 88.7 us: sum_grads(): pl.pallas_call(functools.partial(reduce_kernel, shards, depth, chunks, ro...]
    all_gather x4 -> x0, waiting for transfers between devices: 110 us -> none  [the longest x1 44.6 us: on_device(): lax.all_gather(input_weight, 'shard', axis=0, tiled=True)]
    reduce_scatter x4 -> x0, waiting for transfers between devices: 102 us -> none  [the longest x1 50.6 us: on_device(): lax.psum_scatter(input_grad.astype(jnp.bfloat16), 'shard', scatter_dimens...]
    psum x1 -> x0, waiting for transfers between devices: 77.9 us -> none  [on_device(): lax.psum(shares[2].astype(jnp.bfloat16), 'replica').astype(jnp.float32)]
    psum x1 -> x0, blocking collectives: 33.7 us -> none  [on_device(): lax.psum(shares[0].astype(jnp.bfloat16), 'replica').astype(jnp.float32)]
    all_gather x2 -> x0, blocking collectives: 9.55 us -> none  [the longest x1 5.22 us: on_device(): lax.all_gather(first_gain, 'shard', axis=0, tiled=True)]
    ppermute x2, waiting for transfers between devices: 15.5 us -> 9.58 us  [extended(): lax.ppermute(head, axis, [((i + 1) % count, i) for i in range(ends)])]
    convert_element_type x7 -> x2, other arithmetic: 9.19 us -> 3.95 us  [the longest x1 2.64 us: sum_grads(): parts.append(total[start:start + size].astype(jnp.float32))]
  transfers between devices with their start and end apart: 13 -> 4, of which waited for: 11 -> 3; matrix products, arithmetic and copies ran while one was open for 13% -> 3% of each run, Pallas kernels for 0% -> 0%
where the time goes in v1:
time: 261 us; the launch traced here: 260 us
  Pallas kernels  135 us (52%)
  local copies, waits for them, and re-layouts  35.9 us (14%)
  other arithmetic  31 us (12%)
  matrix products  30 us (11%)
  waiting for transfers between devices  19.5 us (7%)
  starting transfers between devices  7.26 us (3%)
    pallas_call x1, Pallas kernels, sum_grads(): pl.pallas_call(functools.partial(reduce_kernel, shards, depth, chunks, ro...  88.7 us
    pallas_call x1, Pallas kernels, gather_weights(): pl.pallas_call(functools.partial(gather_kernel, shards, splits), out_shap...  46.3 us
    unnamed x124, local copies, waits for them, and re-layouts  19 us
    ppermute x2, waiting for transfers between devices, extended(): lax.ppermute(tail, axis, [(i, (i + 1) % count) for i in range(ends)])  9.88 us
    ppermute x2, waiting for transfers between devices, extended(): lax.ppermute(head, axis, [((i + 1) % count, i) for i in range(ends)])  9.58 us
  transfers between devices with their start and end apart: 4, of which 3 were waited for; matrix products, arithmetic and copies ran while one was open for 3% of the time, Pallas kernels for 0%

profile of v1, /device:TPU:0, one launch (start us, length us, event | category | flops | bytes accessed | tf_op | source)
XLA Modules:
  0.0 259.9 jit_solution(16414074736196719628)
XLA Ops:
  0.6 0.7 pad_maximum_fusion.11
  1.4 1.5 copy-done.2
  2.9 1.5 copy-done.3
  4.3 1.2 copy-done.7
  5.5 1.1 copy-done.8
  6.6 46.3 %gather_weights.1 = (bf16[2,16,768]{2,1,0:T(8,128)(2,1)S(1)}, bf16[2,384,2304]{2,1,0:T(8,128)(2,1)S(1)}, bf16[2,384,768]{2,1,0:T(8,128)(2,1)S(1)}, bf16[2,384,2304]{2,1,0:T(8,128)(2,1)}, bf16[2,576,768]{2,1,0:T(8,128)(2,1)S(1)}) custom-call(bf16[16,768]{1,0:T(8,128)(2,1)S(1)} %pad.20.refs_0_, bf16[384,2304]{1,0:T(8,128)(2,1)S(1)} %copy-done.2, ...), custom_call_target="tpu_custom_call" | custom-call | tf_op jit(solution)/shard_map/gather_weights/pallas_call | solution.py:188
  52.8 1.8 copy-done
  54.6 1.2 copy-done.4
  56.3 3.1 %fusion.52 = f32[256,2304]{1,0:T(8,128)S(1)} fusion(bf16[768,2304]{1,0:T(8,128)(2,1)} %bitcast.61, bf16[256,768]{1,0:T(8,128)(2,1)S(1)} %copy-done.12, f32[768]{0:T(1024)S(1)} %reshape.361, f32[256]{0:T(256)S(1)} %fusion.45, f32[256]{0:T(256)S(1)} %broadcast_multiply_fusion.6), kind=kOutput, calls=%fused_computation.140 | convolution fusion | flops 906952704 | bytes 6296576 | tf_op jit(solution)/shard_map/dot_general | solution.py:460
  59.5 1.0 slice.134
  61.2 1.5 copy.33
  63.5 0.8 broadcast_multiply_fusion.3
  64.4 1.1 copy.34
  65.6 1.1 copy.32
  66.8 2.9 %fusion.59 = (f32[256,768]{1,0:T(8,128)}, bf16[256,768]{1,0:T(8,128)(2,1)S(1)}) fusion(f32[256,2304]{1,0:T(8,128)} %copy-done.14, f32[256,768]{1,0:T(8,128)} %copy.34, f32[256,768]{1,0:T(8,128)} %copy.32), kind=kLoop, calls=%fused_computation.145 | loop fusion | flops 589824 | bytes 4325376 | tf_op jit(solution)/shard_map/slice | solution.py:462
  69.7 0.8 pad_maximum_fusion.9
  70.4 2.5 collective-permute-start
  72.9 1.3 collective-permute-start.1
  74.2 1.4 copy.36
  75.6 0.8 slice_negate_fusion.2
  76.5 1.9 fusion.29
  79.3 4.7 %collective-permute-done.1 = bf16[64,1536]{1,0:T(8,128)(2,1)} collective-permute-done((bf16[64,1536]{1,0:T(8,128)(2,1)}, bf16[64,1536]{1,0:T(8,128)(2,1)}, u32[]{:S(2)}, u32[]{:S(2)}) %collective-permute-start.1) | collective-permute-done | bytes 196640 | tf_op jit(solution)/shard_map/ppermute | solution.py:32
  84.1 1.2 pad_maximum_fusion.1
  85.2 0.9 fusion.62
  86.5 1.6 copy.35
  88.1 1.0 fusion.65
  89.1 1.5 fusion
  91.2 1.7 fusion.10
  93.9 1.4 copy-done.25
  95.4 1.1 fusion.55
  96.9 3.1 %add_convert_fusion = (bf16[256,1152]{1,0:T(8,128)(2,1)S(1)}, f32[256,1152]{1,0:T(8,128)S(1)}, f32[256,1152]{1,0:T(8,128)S(1)}) fusion(f32[256,2304]{1,0:T(8,128)S(1)} %fusion.55, bf16[1152,768]{1,0:T(8,128)(2,1)S(1)} %bitcast.63, bf16[256,768]{1,0:T(8,128)(2,1)S(1)} %copy-done.28), kind=kOutput, calls=%fused_computation.45 | convolution fusion | flops 474513408 | bytes 7471104 | tf_op jit(solution)/shard_map/td,fd->tf/dot_general | solution.py:495
  100.0 1.1 multiply_convert_fusion.1
  101.1 1.3 multiply_reduce_fusion.1
  102.9 0.7 copy-done.19
  104.3 3.7 %multiply_reduce_fusion = (f32[12,256]{1,0:T(8,128)S(1)}, f32[12,256,384]{2,1,0:T(8,128)S(1)}) fusion(f32[12,256,384]{2,1,0:T(8,128)} %copy-done.9, f32[12,256]{1,0:T(8,128)S(1)} %log_add_fusion, bf16[256,12,64]{0,2,1:T(8,128)(2,1)S(1)} %bitcast.78, bf16[384,12,64]{0,2,1:T(8,128)(2,1)} %bitcast.87), kind=kOutput, calls=%fused_computation.3 | convolution fusion | flops 154530816 | bytes 10444800 | tf_op jit(solution)/shard_map/qhd,khd->hqk/dot_general | solution.py:525
  108.1 1.4 fusion.3
  109.5 3.1 %convolution_convert_fusion = bf16[768,2304]{1,0:T(8,128)(2,1)} fusion(bf16[256,1152]{1,0:T(8,128)(2,1)S(1)} %get-tuple-element.37, bf16[256,1152]{1,0:T(8,128)(2,1)S(1)} %copy-done.44, f32[256,768]{1,0:T(8,128)S(1)} %copy-done.11, f32[768]{0:T(1024)S(1)} %copy-done.48, f32[256]{0:T(256)S(1)} %fusion.46, f32[256]{0:T(256)S(1)} %broadcast_multiply_fusion.5), kind=kOutput, calls=%fused_computation | convolution fusion | flops 910884864 | bytes 5510144 | tf_op jit(solution)/shard_map/td,tf->df/dot_general | solution.py:498
  113.8 0.7 convolution_convert_fusion.2
  114.4 0.8 copy-done.6
  115.2 1.4 fusion.9
  116.7 1.1 multiply_convert_fusion
  118.9 2.0 broadcast_multiply_fusion
  121.1 1.0 fusion.61
  122.0 2.2 collective-permute-start.2
  124.2 1.3 collective-permute-start.3
  125.5 2.1 fusion.63
  127.6 9.9 %collective-permute-done.2 = bf16[64,1536]{0,1:T(8,128)(2,1)} collective-permute-done((bf16[64,1536]{0,1:T(8,128)(2,1)}, bf16[64,1536]{0,1:T(8,128)(2,1)}, u32[]{:S(2)}, u32[]{:S(2)}) %collective-permute-start.2) | collective-permute-done | bytes 196640 | tf_op jit(solution)/shard_map/ppermute | solution.py:30
  137.5 4.8 %collective-permute-done.3 = bf16[64,1536]{0,1:T(8,128)(2,1)} collective-permute-done((bf16[64,1536]{0,1:T(8,128)(2,1)S(1)}, bf16[64,1536]{0,1:T(8,128)(2,1)}, u32[]{:S(2)}, u32[]{:S(2)}) %collective-permute-start.3) | collective-permute-done | bytes 196640 | tf_op jit(solution)/shard_map/ppermute | solution.py:32
  142.3 0.8 broadcast_in_dim.58
  143.1 3.6 %concatenate.69 = bf16[384,1536]{0,1:T(8,128)(2,1)} concatenate(bf16[64,1536]{0,1:T(8,128)(2,1)} %collective-permute-done.2, bf16[64,1536]{0,1:T(8,128)(2,1)S(1)} %get-tuple-element.43, bf16[128,1536]{0,1:T(8,128)(2,1)} %broadcast_in_dim.58, bf16[64,1536]{0,1:T(8,128)(2,1)} %get-tuple-element.44, bf16[64,1536]{0,1:T(8,128)(2,1)} %collective-permute-done.3), dimensions={0} | concatenate | bytes 2359296 | tf_op jit(solution)/shard_map/concatenate | solution.py:28
  146.8 1.5 fusion.60
  148.6 0.7 fusion.8
  149.5 0.7 copy-done.42
  150.4 1.0 copy-done.33
  152.0 1.6 copy-done.1
  153.7 1.2 fusion.27
  154.9 3.1 %convolution_convert_fusion.1 = bf16[768,2304]{1,0:T(8,128)(2,1)} fusion(bf16[256,768]{0,1:T(8,128)(2,1)S(1)} %slice.188, bf16[256,768]{0,1:T(8,128)(2,1)S(1)} %bitcast.91, bf16[256,768]{0,1:T(8,128)(2,1)S(1)} %bitcast.93, bf16[256,768]{1,0:T(8,128)(2,1)S(1)} %copy-done.13, f32[768]{0:T(1024)S(1)} %copy-done.50, f32[256]{0:T(256)S(1)} %copy-done.54, ...), kind=kOutput, calls=%fused_computation.1 | convolution fusion | flops 912261120 | bytes 5116928 | tf_op jit(solution)/shard_map/td,te->de/dot_general | solution.py:554
  158.5 88.7 %reduce_terms.1 = bf16[3328,768]{1,0:T(8,128)(2,1)} custom-call(bf16[2,384,2304]{2,1,0:T(8,128)(2,1)} %bitcast.80, bf16[2,384,768]{2,1,0:T(8,128)(2,1)S(1)} %bitcast.58, bf16[2,384,2304]{2,1,0:T(8,128)(2,1)} %bitcast.67, bf16[2,576,768]{2,1,0:T(8,128)(2,1)S(1)} %bitcast.57, bf16[2,16,768]{2,1,0:T(8,128)(2,1)S(1)} %fusion.42.refs_4_), custom_call_target="tpu_custom_call" | custom-call | tf_op jit(solution)/shard_map/reduce_terms/pallas_call | solution.py:394
  247.2 3.5 %fusion.58 = (bf16[384,768]{1,0:T(8,128)(2,1)S(1)}, bf16[384,768]{1,0:T(8,128)(2,1)S(1)}, bf16[384,768]{1,0:T(8,128)(2,1)S(1)}, f32[384,768]{1,0:T(8,128)}, bf16...) fusion(bf16[3328,768]{1,0:T(8,128)(2,1)} %reduce_terms.1), kind=kLoop, calls=%fused_computation.144 | loop fusion | flops 294912 | bytes 8847360 | tf_op jit(solution)/shard_map/slice | solution.py:419
  250.7 2.6 %slice_convert_fusion = f32[576,768]{1,0:T(8,128)} fusion(bf16[3328,768]{1,0:T(8,128)(2,1)} %reduce_terms.1), kind=kLoop, calls=%fused_computation.64 | loop fusion | flops 442368 | bytes 2654208 | tf_op jit(solution)/shard_map/convert_element_type | solution.py:419
  253.3 1.3 convert_reduce_fusion.3
  254.6 1.3 add_add_fusion.2
  255.9 2.0 maximum_convert_fusion.1
  257.9 2.0 maximum_convert_fusion
  (162 shorter events, 10.6 us)
Async XLA Ops:
  1.4 1.5 copy-start.2
  2.9 1.5 copy-start.3
  4.3 1.2 copy-start.7
  5.5 1.1 copy-start.8
  6.6 49.3 %copy-start.12 = (bf16[256,768]{1,0:T(8,128)(2,1)S(1)}, bf16[256,768]{1,0:T(8,128)(2,1)}, u32[]{:S(2)}) copy-start(bf16[256,768]{1,0:T(8,128)(2,1)} %param.10) | copy-start | bytes 1179652
  52.8 1.8 copy-start
  54.6 1.2 copy-start.4
  55.9 3.6 %copy-start.49 = (f32[768]{0:T(1024)}, f32[768]{0:T(1024)S(1)}, u32[]{:S(2)}) copy-start(f32[768]{0:T(1024)S(1)} %reshape.361) | copy-start | bytes 9220
  56.0 3.5 %copy-start.51 = (f32[256]{0:T(256)}, f32[256]{0:T(256)S(1)}, u32[]{:S(2)}) copy-start(f32[256]{0:T(256)S(1)} %broadcast_multiply_fusion.6) | copy-start | bytes 3076
  56.3 3.2 %copy-start.55 = (f32[256]{0:T(256)}, f32[256]{0:T(256)S(1)}, u32[]{:S(2)}) copy-start(f32[256]{0:T(256)S(1)} %fusion.26) | copy-start | bytes 3076
  56.3 3.2 %copy-start.53 = (f32[256]{0:T(256)}, f32[256]{0:T(256)S(1)}, u32[]{:S(2)}) copy-start(f32[256]{0:T(256)S(1)} %fusion.45) | copy-start | bytes 3076
  59.5 1.7 copy-start.14
  61.2 8.4 %copy-start.24 = (bf16[256,768]{1,0:T(8,128)(2,1)}, bf16[256,768]{1,0:T(8,128)(2,1)S(1)}, u32[]{:S(2)}) copy-start(bf16[256,768]{1,0:T(8,128)(2,1)S(1)} %slice.189) | copy-start | bytes 1179652
  64.3 12.2 %copy-start.39 = (f32[256,64]{0,1:T(8,128)}, f32[256,64]{0,1:T(8,128)S(1)}, u32[]{:S(2)}) copy-start(f32[256,64]{0,1:T(8,128)S(1)} %get-tuple-element.60) | copy-start | bytes 196612
  64.3 12.2 %copy-start.41 = (f32[256,64]{0,1:T(8,128)}, f32[256,64]{0,1:T(8,128)S(1)}, u32[]{:S(2)}) copy-start(f32[256,64]{0,1:T(8,128)S(1)} %get-tuple-element.59) | copy-start | bytes 196612
  70.4 8.9 %collective-permute-start = (bf16[64,1536]{1,0:T(8,128)(2,1)}, bf16[64,1536]{1,0:T(8,128)(2,1)S(1)}, u32[]{:S(2)}, u32[]{:S(2)}) collective-permute-start(bf16[64,1536]{1,0:T(8,128)(2,1)} %get-tuple-element.53), channel_id=1, source_target_pairs={{0,1},{1,2},{2,3},{3,4},{4,5},{5,6},{6,7},{7,8},{8,9},{9,10},{10,1... | collective-permute-start | bytes 589832 | tf_op jit(solution)/shard_map/ppermute | solution.py:30
  72.9 11.1 %collective-permute-start.1 = (bf16[64,1536]{1,0:T(8,128)(2,1)}, bf16[64,1536]{1,0:T(8,128)(2,1)}, u32[]{:S(2)}, u32[]{:S(2)}) collective-permute-start(bf16[64,1536]{1,0:T(8,128)(2,1)} %get-tuple-element.54), channel_id=1, source_target_pairs={{1,0},{2,1},{3,2},{4,3},{5,4},{6,5},{7,6},{8,7},{9,8},{10,9},{11,1... | collective-permute-start | bytes 589832 | tf_op jit(solution)/shard_map/ppermute | solution.py:32
  76.5 2.6 copy-start.59
  76.5 17.4 %copy-start.47 = (f32[768]{0:T(1024)}, f32[768]{0:T(1024)S(1)}, u32[]{:S(2)}) copy-start(f32[768]{0:T(1024)S(1)} %reshape.362) | copy-start | bytes 9220
  86.1 1.9 copy-start.26
  86.4 2.6 %copy-start.22 = (bf16[384,768]{0,1:T(8,128)(2,1)}, bf16[384,768]{0,1:T(8,128)(2,1)S(1)}, u32[]{:S(2)}) copy-start(bf16[384,768]{0,1:T(8,128)(2,1)S(1)} %copy.37) | copy-start | bytes 1769476
  88.0 2.6 copy-start.34
  89.1 2.1 copy-start.9
  93.0 2.4 copy-start.25
  93.7 8.7 %copy-start.10 = (f32[256,768]{1,0:T(8,128)}, f32[256,768]{1,0:T(8,128)S(1)}, u32[]{:S(2)}) copy-start(f32[256,768]{1,0:T(8,128)S(1)} %get-tuple-element.64) | copy-start | bytes 2359300
  95.4 1.5 copy-start.5
  95.4 1.5 copy-start.28
  100.0 1.1 copy-start.43
  100.0 1.1 copy-start.48
  102.7 0.9 copy-start.19
  104.1 3.9 %slice-start = ((s8[4718592]{0:T(1024)(128)(4,1)}), s8[524288]{0:T(1024)(128)(4,1)S(1)}, s32[]{:S(2)}) async-start(s8[4718592]{0:T(1024)(128)(4,1)} %bitcast.65), calls=%async_computation | async-start | bytes 1048576
  104.3 3.8 %slice-start.1 = ((s8[4718592]{0:T(1024)(128)(4,1)}), s8[4194304]{0:T(1024)(128)(4,1)S(1)}, s32[]{:S(2)}) async-start(s8[4718592]{0:T(1024)(128)(4,1)} %bitcast.65), calls=%async_computation.1 | async-start | bytes 8388608
  108.1 1.4 copy-start.11
  108.1 1.4 copy-start.44
  109.5 11.4 %copy-start.15 = (f32[12,64,384]{2,1,0:T(8,128)}, f32[12,64,384]{2,1,0:T(8,128)S(1)}, u32[]{:S(2)}) copy-start(f32[12,64,384]{2,1,0:T(8,128)S(1)} %fusion.3) | copy-start | bytes 3538948
  109.5 3.1 %copy-start.36 = (bf16[12,64,256]{2,1,0:T(8,128)(2,1)S(1)}, bf16[12,64,256]{2,1,0:T(8,128)(2,1)}, u32[]{:S(2)}) copy-start(bf16[12,64,256]{2,1,0:T(8,128)(2,1)} %copy-done.35) | copy-start | bytes 1179652
  112.6 1.1 copy-start.21
  112.6 1.2 copy-start.29
  113.8 1.5 copy-start.6
  116.7 1.1 copy-start.27
  117.8 1.1 copy-start.23
  117.9 1.1 copy-start.46
  118.3 2.6 %copy-start.17 = (f32[12,64,384]{2,1,0:T(8,128)}, f32[12,64,384]{2,1,0:T(8,128)S(1)}, u32[]{:S(2)}) copy-start(f32[12,64,384]{2,1,0:T(8,128)S(1)} %convolution_multiply_fusion) | copy-start | bytes 3538948
  122.0 15.5 %collective-permute-start.2 = (bf16[64,1536]{0,1:T(8,128)(2,1)}, bf16[64,1536]{0,1:T(8,128)(2,1)}, u32[]{:S(2)}, u32[]{:S(2)}) collective-permute-start(bf16[64,1536]{0,1:T(8,128)(2,1)} %get-tuple-element.44), channel_id=1, source_target_pairs={{0,1},{1,2},{2,3},{3,4},{4,5},{5,6},{6,7},{7,8},{8,9},{9,10},{10,1... | collective-permute-start | bytes 589832 | tf_op jit(solution)/shard_map/ppermute | solution.py:30
  124.2 18.1 %collective-permute-start.3 = (bf16[64,1536]{0,1:T(8,128)(2,1)S(1)}, bf16[64,1536]{0,1:T(8,128)(2,1)}, u32[]{:S(2)}, u32[]{:S(2)}) collective-permute-start(bf16[64,1536]{0,1:T(8,128)(2,1)S(1)} %get-tuple-element.43), channel_id=1, source_target_pairs={{1,0},{2,1},{3,2},{4,3},{5,4},{6,5},{7,6},{8,7},{9,8},{10,9},{11,1... | collective-permute-start | bytes 589832 | tf_op jit(solution)/shard_map/ppermute | solution.py:32
  146.8 1.5 copy-start.16
  146.8 1.9 copy-start.18
  146.8 1.9 copy-start.58
  149.3 0.8 copy-start.42
  149.4 1.0 copy-start.40
  149.4 1.0 copy-start.45
  150.3 1.1 copy-start.33
  150.3 1.2 copy-start.37
  150.3 1.3 copy-start.38
  151.6 2.0 copy-start.1
  151.6 2.1 copy-start.13
  151.6 2.1 copy-start.50
  151.6 2.1 copy-start.52
  153.7 1.2 copy-start.54
  154.9 3.1 %copy-start.31 = (f32[256,768]{1,0:T(8,128)}, f32[256,768]{1,0:T(8,128)S(1)}, u32[]{:S(2)}) copy-start(f32[256,768]{1,0:T(8,128)S(1)} %get-tuple-element.72) | copy-start | bytes 2359300
  154.9 3.1 %copy-start.56 = (f32[256]{0:T(256)S(1)}, f32[256]{0:T(256)}, u32[]{:S(2)}) copy-start(f32[256]{0:T(256)} %copy-done.55) | copy-start | bytes 3076
  250.7 4.0 %copy-start.20 = (f32[256,768]{1,0:T(8,128)S(1)}, f32[256,768]{1,0:T(8,128)}, u32[]{:S(2)}) copy-start(f32[256,768]{1,0:T(8,128)} %copy-done.19) | copy-start | bytes 2359300
  250.7 4.0 %copy-start.30 = (bf16[256,768]{1,0:T(8,128)(2,1)S(1)}, bf16[256,768]{1,0:T(8,128)(2,1)}, u32[]{:S(2)}) copy-start(bf16[256,768]{1,0:T(8,128)(2,1)} %param.11) | copy-start | bytes 1179652
  250.7 4.0 %copy-start.32 = (f32[256,768]{1,0:T(8,128)S(1)}, f32[256,768]{1,0:T(8,128)}, u32[]{:S(2)}) copy-start(f32[256,768]{1,0:T(8,128)} %copy-done.31) | copy-start | bytes 2359300
  (2 other events, 1.4 us)

commit v2 on v1

--- a/solution.py
+++ b/solution.py
@@ -77,7 +77,7 @@
     return allowed
 
 
-PACK = 768
+PACK = 384
 UNIT = 16
 MESH = pl.DeviceIdType.MESH
 
@@ -215,8 +215,8 @@
                 packs.at[len(loads)],
             )
             load.start()
-            loads.append(load)
             filled += taken
+            loads.append((load, filled))
     if filled < chunks * rows:
         terms[:, filled:, :] = jnp.zeros((shards, chunks * rows - filled, PACK), terms.dtype)
     replica = lax.axis_index("replica")
@@ -231,8 +231,6 @@
     levels = [lax.rem(level + off, depth) for off in range(1, depth)]
     deep_peers = [(4 * other + lax.rem(replica, 4), me) for other in levels]
     greet([core_peer, side_peer] + shard_peers + deep_peers)
-    for load in loads:
-        load.wait()
     first_shard, first_side, first_deep = 1, shards, shards + 1
     back_deep, back_side, back_core = shards + depth, shards + 2 * depth - 1, shards + 2 * depth
 
@@ -306,9 +304,6 @@
         for one in copies:
             one.wait_recv()
 
-    def step_start(k):
-        begin(to_core(k))
-
     def step_core(k):
         arrive(to_core(k))
         own = terms[:, span(k * rows + core * half, half), :]
@@ -353,7 +348,6 @@
                 one.wait_send()
 
     steps = (
-        step_start,
         step_core,
         step_shard,
         step_side,
@@ -373,6 +367,14 @@
 
         return carry
 
+    sent = 0
+    for load, ready in loads:
+        load.wait()
+        while (sent + 1) * rows <= ready:
+            begin(to_core(sent))
+            sent += 1
+    for k in range(sent, chunks):
+        begin(to_core(k))
     lax.fori_loop(0, chunks + len(steps) - 1, tick, 0)
 
 
@@ -382,8 +384,9 @@
         for matrix in matrices
     ]
     if gains:
-        line = jnp.concatenate([g.astype(jnp.bfloat16).reshape(shards, 1, -1) for g in gains], 2)
-        blocks.append(jnp.pad(line, ((0, 0), (0, UNIT - 1), (0, PACK - line.shape[2]))))
+        lines = jnp.concatenate([g.astype(jnp.bfloat16).reshape(shards, 1, -1) for g in gains], 1)
+        short = (UNIT - len(gains), PACK - lines.shape[2])
+        blocks.append(jnp.pad(lines, ((0, 0), (0, short[0]), (0, short[1]))))
     pieces = [block.shape[1] for block in blocks for _ in range(0, block.shape[2], PACK)]
     rows = UNIT * replicas
     chunks = -(-sum(pieces) // rows)
@@ -421,7 +424,7 @@
         results.append(jnp.concatenate(parts, 1))
     for i, gain in enumerate(gains):
         size = gain.shape[0] // shards
-        results.append(total[start, i * size : (i + 1) * size].astype(jnp.float32))
+        results.append(total[start + i, :size].astype(jnp.float32))
     return results
 
 

time: 261 us -> 298 us (1.14)
  Pallas kernels: 135 us -> 155 us
  local copies, waits for them, and re-layouts: 35.9 us -> 51.1 us
  waiting for transfers between devices: 19.5 us -> 16.3 us
    pallas_call x1, Pallas kernels: 88.7 us -> 109 us  [sum_grads(): pl.pallas_call(functools.partial(reduce_kernel, shards, depth, chunks, ro...]
    unnamed x124 -> x147, local copies, waits for them, and re-layouts: 19 us -> 23.2 us
    slice x1 -> x0, other arithmetic: 3.47 us -> none  [sum_grads(): parts.append(total[start:start + size].astype(jnp.float32))]
    ppermute x2, waiting for transfers between devices: 9.58 us -> 6.31 us  [extended(): lax.ppermute(head, axis, [((i + 1) % count, i) for i in range(ends)])]
    mul x3, local copies, waits for them, and re-layouts: 2.36 us -> 5.54 us  [rotate(): return values * cosine + turned * sine]
    concatenate x2 -> x4, other arithmetic: 4.04 us -> 6.47 us  [sum_grads(): results.append(jnp.concatenate(parts, 1))]
where the time goes in v2:
time: 298 us; the launch traced here: 297 us
  Pallas kernels  155 us (52%)
  local copies, waits for them, and re-layouts  51.1 us (17%)
  matrix products  31.7 us (11%)
  other arithmetic  31.2 us (10%)
  waiting for transfers between devices  16.3 us (5%)
  starting transfers between devices  9.58 us (3%)
    pallas_call x1, Pallas kernels, sum_grads(): pl.pallas_call(functools.partial(reduce_kernel, shards, depth, chunks, ro...  109 us
    pallas_call x1, Pallas kernels, gather_weights(): pl.pallas_call(functools.partial(gather_kernel, shards, splits), out_shap...  46.2 us
    unnamed x147, local copies, waits for them, and re-layouts  23.2 us
    ppermute x2, waiting for transfers between devices, extended(): lax.ppermute(tail, axis, [(i, (i + 1) % count) for i in range(ends)])  9.95 us
    ppermute x2, starting transfers between devices, extended(): lax.ppermute(tail, axis, [(i, (i + 1) % count) for i in range(ends)])  7.02 us
    concatenate x4, other arithmetic, sum_grads(): results.append(jnp.concatenate(parts, 1))  6.47 us
    ppermute x2, waiting for transfers between devices, extended(): lax.ppermute(head, axis, [((i + 1) % count, i) for i in range(ends)])  6.31 us
  transfers between devices with their start and end apart: 4, of which 3 were waited for; matrix products, arithmetic and copies ran while one was open for 3% of the time, Pallas kernels for 0%

profile of v2, /device:TPU:0, one launch (start us, length us, event | category | flops | bytes accessed | tf_op | source)
XLA Modules:
  0.0 296.5 jit_solution(1331544076187029173)
XLA Ops:
  1.4 1.5 copy-done.2
  2.9 1.5 copy-done.3
  4.3 1.2 copy-done.6
  5.5 1.1 copy-done.7
  6.6 46.2 %gather_weights.1 = (bf16[2,16,768]{2,1,0:T(8,128)(2,1)S(1)}, bf16[2,384,2304]{2,1,0:T(8,128)(2,1)S(1)}, bf16[2,384,768]{2,1,0:T(8,128)(2,1)S(1)}, bf16[2,384,2304]{2,1,0:T(8,128)(2,1)}, bf16[2,576,768]{2,1,0:T(8,128)(2,1)S(1)}) custom-call(bf16[16,768]{1,0:T(8,128)(2,1)S(1)} %pad.20.refs_0_, bf16[384,2304]{1,0:T(8,128)(2,1)S(1)} %copy-done.2, ...), custom_call_target="tpu_custom_call" | custom-call | tf_op jit(solution)/shard_map/gather_weights/pallas_call | solution.py:188
  52.8 1.8 copy-done
  55.1 3.3 %fusion.52 = f32[256,2304]{1,0:T(8,128)S(1)} fusion(bf16[768,2304]{1,0:T(8,128)(2,1)} %bitcast.61, bf16[256,768]{1,0:T(8,128)(2,1)S(1)} %copy-done.11, f32[768]{0:T(1024)S(1)} %reshape.361, f32[256]{0:T(256)S(1)} %fusion.45, f32[256]{0:T(256)S(1)} %broadcast_multiply_fusion.6), kind=kOutput, calls=%fused_computation.150 | convolution fusion | flops 906952704 | bytes 6296576 | tf_op jit(solution)/shard_map/dot_general | solution.py:463
  58.4 1.0 slice.166
  60.9 2.3 copy.33
  63.2 1.2 slice_negate_fusion.3
  66.2 2.3 copy.34
  68.5 0.9 mul.276
  69.4 2.3 copy.32
  71.7 2.9 fusion.59
  76.2 3.2 %collective-permute-start = (bf16[64,1536]{1,0:T(8,128)(2,1)}, bf16[64,1536]{1,0:T(8,128)(2,1)}, u32[]{:S(2)}, u32[]{:S(2)}) collective-permute-start(bf16[64,1536]{1,0:T(8,128)(2,1)} %get-tuple-element.62), channel_id=1, source_target_pairs={{0,1},{1,2},{2,3},{3,4},{4,5},{5,6},{6,7},{7,8},{8,9},{9,10},{10,1... | collective-permute-start | bytes 589832 | tf_op jit(solution)/shard_map/ppermute | solution.py:30
  79.4 1.3 collective-permute-start.1
  80.7 2.3 copy.36
  83.0 2.1 slice_negate_fusion.2
  85.1 2.3 fusion.29
  88.3 1.5 collective-permute-done.1
  89.8 1.1 pad_maximum_fusion.1
  90.9 1.1 fusion.62
  92.0 2.1 copy.37
  94.2 2.1 copy.35
  96.3 2.2 fusion.65
  98.5 1.5 fusion
  100.7 1.7 fusion.10
  103.3 1.6 copy-done.25
  104.8 1.1 fusion.55
  106.0 3.1 %add_convert_fusion = (bf16[256,1152]{1,0:T(8,128)(2,1)S(1)}, f32[256,1152]{1,0:T(8,128)S(1)}, f32[256,1152]{1,0:T(8,128)S(1)}) fusion(f32[256,2304]{1,0:T(8,128)S(1)} %fusion.55, bf16[1152,768]{1,0:T(8,128)(2,1)S(1)} %bitcast.63, bf16[256,768]{1,0:T(8,128)(2,1)S(1)} %copy-done.27), kind=kOutput, calls=%fused_computation.43 | convolution fusion | flops 474513408 | bytes 7471104 | tf_op jit(solution)/shard_map/td,fd->tf/dot_general | solution.py:498
  109.1 1.1 multiply_convert_fusion.1
  110.2 1.8 multiply_reduce_fusion.1
  114.3 3.7 %multiply_reduce_fusion = (f32[12,256]{1,0:T(8,128)S(1)}, f32[12,256,384]{2,1,0:T(8,128)S(1)}) fusion(f32[12,256,384]{2,1,0:T(8,128)} %copy-done.8, f32[12,256]{1,0:T(8,128)S(1)} %log_add_fusion, bf16[256,12,64]{0,2,1:T(8,128)(2,1)S(1)} %bitcast.80, bf16[384,12,64]{0,2,1:T(8,128)(2,1)S(1)} %bitcast.89), kind=kOutput, calls=%fused_computation.3 | convolution fusion | flops 154530816 | bytes 10444800 | tf_op jit(solution)/shard_map/qhd,khd->hqk/dot_general | solution.py:528
  118.0 1.4 fusion.3
  119.5 3.1 %convolution_convert_fusion = bf16[768,2304]{1,0:T(8,128)(2,1)} fusion(bf16[256,1152]{1,0:T(8,128)(2,1)S(1)} %get-tuple-element.46, bf16[256,1152]{1,0:T(8,128)(2,1)S(1)} %copy-done.44, f32[256,768]{1,0:T(8,128)S(1)} %copy-done.10, f32[768]{0:T(1024)S(1)} %copy-done.48, f32[256]{0:T(256)S(1)} %copy-done.56, f32[256]{0:T(256)S(1)} %copy-done.52), kind=kOutput, calls=%fused_computation | convolution fusion | flops 910884864 | bytes 5510144 | tf_op jit(solution)/shard_map/td,tf->df/dot_general | solution.py:501
  124.6 1.4 fusion.9
  126.1 1.3 multiply_convert_fusion
  128.5 2.0 broadcast_multiply_fusion
  130.6 1.1 fusion.61
  131.7 3.8 %collective-permute-start.2 = (bf16[64,1536]{0,1:T(8,128)(2,1)}, bf16[64,1536]{0,1:T(8,128)(2,1)}, u32[]{:S(2)}, u32[]{:S(2)}) collective-permute-start(bf16[64,1536]{0,1:T(8,128)(2,1)} %get-tuple-element.53), channel_id=1, source_target_pairs={{0,1},{1,2},{2,3},{3,4},{4,5},{5,6},{6,7},{7,8},{8,9},{9,10},{10,1... | collective-permute-start | bytes 589832 | tf_op jit(solution)/shard_map/ppermute | solution.py:30
  135.5 1.3 collective-permute-start.3
  136.8 2.1 fusion.63
  138.9 9.9 %collective-permute-done.2 = bf16[64,1536]{0,1:T(8,128)(2,1)} collective-permute-done((bf16[64,1536]{0,1:T(8,128)(2,1)}, bf16[64,1536]{0,1:T(8,128)(2,1)}, u32[]{:S(2)}, u32[]{:S(2)}) %collective-permute-start.2) | collective-permute-done | bytes 196640 | tf_op jit(solution)/shard_map/ppermute | solution.py:30
  148.8 4.8 %collective-permute-done.3 = bf16[64,1536]{0,1:T(8,128)(2,1)} collective-permute-done((bf16[64,1536]{0,1:T(8,128)(2,1)}, bf16[64,1536]{0,1:T(8,128)(2,1)}, u32[]{:S(2)}, u32[]{:S(2)}) %collective-permute-start.3) | collective-permute-done | bytes 196640 | tf_op jit(solution)/shard_map/ppermute | solution.py:32
  154.5 3.8 %concatenate.81 = bf16[384,1536]{0,1:T(8,128)(2,1)} concatenate(bf16[64,1536]{0,1:T(8,128)(2,1)} %collective-permute-done.2, bf16[64,1536]{0,1:T(8,128)(2,1)} %get-tuple-element.52, bf16[128,1536]{0,1:T(8,128)(2,1)} %broadcast_in_dim.58, bf16[64,1536]{0,1:T(8,128)(2,1)} %get-tuple-element.53, bf16[64,1536]{0,1:T(8,128)(2,1)} %collective-permute-done.3), dimensions={0} | concatenate | bytes 2359296 | tf_op jit(solution)/shard_map/concatenate | solution.py:28
  158.2 1.5 fusion.60
  161.8 0.9 copy-done.32
  163.3 1.6 copy-done.1
  165.0 1.2 fusion.27
  166.2 3.1 %convolution_convert_fusion.1 = bf16[768,2304]{1,0:T(8,128)(2,1)} fusion(bf16[256,768]{0,1:T(8,128)(2,1)S(1)} %slice.230, bf16[256,768]{0,1:T(8,128)(2,1)S(1)} %bitcast.93, bf16[256,768]{0,1:T(8,128)(2,1)S(1)} %bitcast.95, bf16[256,768]{1,0:T(8,128)(2,1)S(1)} %copy-done.11, f32[768]{0:T(1024)S(1)} %copy-done.50, f32[256]{0:T(256)S(1)} %copy-done.58, ...), kind=kOutput, calls=%fused_computation.1 | convolution fusion | flops 912261120 | bytes 5116928 | tf_op jit(solution)/shard_map/td,te->de/dot_general | solution.py:557
  169.8 108.9 %reduce_terms.1 = bf16[6656,384]{1,0:T(8,128)(2,1)} custom-call(bf16[2,384,2304]{2,1,0:T(8,128)(2,1)} %bitcast.84, bf16[2,384,768]{2,1,0:T(8,128)(2,1)S(1)} %bitcast.60, bf16[2,384,2304]{2,1,0:T(8,128)(2,1)} %bitcast.69, bf16[2,576,768]{2,1,0:T(8,128)(2,1)S(1)} %bitcast.57, bf16[2,16,384]{2,1,0:T(8,128)(2,1)S(1)} %fusion.42.refs_4_), custom_call_target="tpu_custom_call" | custom-call | tf_op jit(solution)/shard_map/reduce_terms/pallas_call | solution.py:397
  278.7 1.2 fusion.58
  279.9 1.1 slice_dynamic-update-slice_fusion.5
  281.1 1.4 convert_reduce_fusion.3
  282.4 1.2 slice_dynamic-update-slice_fusion.4
  283.6 1.2 slice_dynamic-update-slice_fusion.3
  284.7 1.2 slice_dynamic-update-slice_fusion.2
  285.9 1.2 slice_dynamic-update-slice_fusion.1
  287.1 1.4 slice_dynamic-update-slice_fusion
  288.5 2.0 concatenate.86
  290.5 2.0 concatenate.90
  292.8 1.3 add_add_fusion.2
  294.1 1.3 maximum_convert_fusion
  295.4 1.1 maximum_convert_fusion.1
  (188 shorter events, 18.1 us)
Async XLA Ops:
  1.4 1.5 copy-start.2
  2.9 1.5 copy-start.3
  4.3 1.2 copy-start.6
  6.6 48.1 %copy-start.11 = (bf16[256,768]{1,0:T(8,128)(2,1)S(1)}, bf16[256,768]{1,0:T(8,128)(2,1)}, u32[]{:S(2)}) copy-start(bf16[256,768]{1,0:T(8,128)(2,1)} %param.10) | copy-start | bytes 1179652
  52.8 1.8 copy-start
  54.6 51.4 %copy-start.4 = (bf16[2,576,768]{2,1,0:T(8,128)(2,1)}, bf16[2,576,768]{2,1,0:T(8,128)(2,1)S(1)}, u32[]{:S(2)}) copy-start(bf16[2,576,768]{2,1,0:T(8,128)(2,1)S(1)} %get-tuple-element.17) | copy-start | bytes 5308420
  54.7 3.7 %copy-start.49 = (f32[768]{0:T(1024)}, f32[768]{0:T(1024)S(1)}, u32[]{:S(2)}) copy-start(f32[768]{0:T(1024)S(1)} %reshape.361) | copy-start | bytes 9220
  54.8 3.6 %copy-start.53 = (f32[256]{0:T(256)}, f32[256]{0:T(256)S(1)}, u32[]{:S(2)}) copy-start(f32[256]{0:T(256)S(1)} %broadcast_multiply_fusion.6) | copy-start | bytes 3076
  55.1 3.3 %copy-start.59 = (f32[256]{0:T(256)}, f32[256]{0:T(256)S(1)}, u32[]{:S(2)}) copy-start(f32[256]{0:T(256)S(1)} %fusion.26) | copy-start | bytes 3076
  55.1 3.3 %copy-start.57 = (f32[256]{0:T(256)}, f32[256]{0:T(256)S(1)}, u32[]{:S(2)}) copy-start(f32[256]{0:T(256)S(1)} %fusion.45) | copy-start | bytes 3076
  58.4 1.7 copy-start.12
  60.9 3.5 %copy-start.63 = (s32[256]{0:T(256)S(1)}, s32[256]{0:T(256)}, u32[]{:S(2)}) copy-start(s32[256]{0:T(256)} %param.12) | copy-start | bytes 3076
  65.3 19.9 %copy-start.39 = (f32[256,64]{0,1:T(8,128)}, f32[256,64]{0,1:T(8,128)S(1)}, u32[]{:S(2)}) copy-start(f32[256,64]{0,1:T(8,128)S(1)} %get-tuple-element.69) | copy-start | bytes 196612
  65.3 19.9 %copy-start.41 = (f32[256,64]{0,1:T(8,128)}, f32[256,64]{0,1:T(8,128)S(1)}, u32[]{:S(2)}) copy-start(f32[256,64]{0,1:T(8,128)S(1)} %get-tuple-element.68) | copy-start | bytes 196612
  71.7 3.7 %copy-start.23 = (bf16[256,768]{1,0:T(8,128)(2,1)S(1)}, bf16[256,768]{1,0:T(8,128)(2,1)}, u32[]{:S(2)}) copy-start(bf16[256,768]{1,0:T(8,128)(2,1)} %slice.231) | copy-start | bytes 1179652
  76.2 12.1 %collective-permute-start = (bf16[64,1536]{1,0:T(8,128)(2,1)}, bf16[64,1536]{1,0:T(8,128)(2,1)}, u32[]{:S(2)}, u32[]{:S(2)}) collective-permute-start(bf16[64,1536]{1,0:T(8,128)(2,1)} %get-tuple-element.62), channel_id=1, source_target_pairs={{0,1},{1,2},{2,3},{3,4},{4,5},{5,6},{6,7},{7,8},{8,9},{9,10},{10,1... | collective-permute-start | bytes 589832 | tf_op jit(solution)/shard_map/ppermute | solution.py:30
  79.4 10.5 %collective-permute-start.1 = (bf16[64,1536]{1,0:T(8,128)(2,1)}, bf16[64,1536]{1,0:T(8,128)(2,1)}, u32[]{:S(2)}, u32[]{:S(2)}) collective-permute-start(bf16[64,1536]{1,0:T(8,128)(2,1)} %get-tuple-element.63), channel_id=1, source_target_pairs={{1,0},{2,1},{3,2},{4,3},{5,4},{6,5},{7,6},{8,7},{9,8},{10,9},{11,1... | collective-permute-start | bytes 589832 | tf_op jit(solution)/shard_map/ppermute | solution.py:32
  83.0 5.1 %copy-start.66 = (s32[256]{0:T(256)S(1)}, s32[256]{0:T(256)}, u32[]{:S(2)}) copy-start(s32[256]{0:T(256)} %param.13) | copy-start | bytes 3076
  85.1 26.9 %copy-start.47 = (f32[768]{0:T(1024)}, f32[768]{0:T(1024)S(1)}, u32[]{:S(2)}) copy-start(f32[768]{0:T(1024)S(1)} %reshape.362) | copy-start | bytes 9220
  85.1 4.8 %copy-start.22 = (bf16[256,768]{1,0:T(8,128)(2,1)S(1)}, bf16[256,768]{1,0:T(8,128)(2,1)}, u32[]{:S(2)}) copy-start(bf16[256,768]{1,0:T(8,128)(2,1)} %copy-done.21) | copy-start | bytes 1179652
  85.1 4.7 %copy-start.24 = (bf16[256,768]{1,0:T(8,128)(2,1)S(1)}, bf16[256,768]{1,0:T(8,128)(2,1)}, u32[]{:S(2)}) copy-start(bf16[256,768]{1,0:T(8,128)(2,1)} %slice.231) | copy-start | bytes 1179652
  98.5 2.2 copy-start.8
  98.5 2.2 copy-start.33
  102.4 2.4 copy-start.25
  103.0 8.9 %copy-start.9 = (f32[256,768]{1,0:T(8,128)}, f32[256,768]{1,0:T(8,128)S(1)}, u32[]{:S(2)}) copy-start(f32[256,768]{1,0:T(8,128)S(1)} %get-tuple-element.73) | copy-start | bytes 2359300
  103.0 8.9 %copy-start.51 = (f32[256]{0:T(256)}, f32[256]{0:T(256)S(1)}, u32[]{:S(2)}) copy-start(f32[256]{0:T(256)S(1)} %broadcast_multiply_fusion.5) | copy-start | bytes 3076
  103.3 8.7 %copy-start.55 = (f32[256]{0:T(256)}, f32[256]{0:T(256)S(1)}, u32[]{:S(2)}) copy-start(f32[256]{0:T(256)S(1)} %fusion.46) | copy-start | bytes 3076
  104.8 1.2 copy-start.27
  113.7 4.2 %slice-start = ((s8[4718592]{0:T(1024)(128)(4,1)}), s8[524288]{0:T(1024)(128)(4,1)S(1)}, s32[]{:S(2)}) async-start(s8[4718592]{0:T(1024)(128)(4,1)} %bitcast.65), calls=%async_computation | async-start | bytes 1048576
  114.3 3.7 %slice-start.1 = ((s8[4718592]{0:T(1024)(128)(4,1)}), s8[4194304]{0:T(1024)(128)(4,1)S(1)}, s32[]{:S(2)}) async-start(s8[4718592]{0:T(1024)(128)(4,1)} %bitcast.65), calls=%async_computation.1 | async-start | bytes 8388608
  118.0 1.4 copy-start.10
  118.0 1.4 copy-start.44
  118.0 1.4 copy-start.48
  118.0 1.4 copy-start.52
  118.0 1.4 copy-start.56
  118.0 8.0 %slice-start.2 = ((s8[4718592]{0:T(1024)(128)(4,1)}), s8[4194304]{0:T(1024)(128)(4,1)S(1)}, s32[]{:S(2)}) async-start(s8[4718592]{0:T(1024)(128)(4,1)} %bitcast.67), calls=%async_computation.2 | async-start | bytes 8388608
  119.5 11.0 %copy-start.13 = (f32[12,64,384]{2,1,0:T(8,128)}, f32[12,64,384]{2,1,0:T(8,128)S(1)}, u32[]{:S(2)}) copy-start(f32[12,64,384]{2,1,0:T(8,128)S(1)} %fusion.3) | copy-start | bytes 3538948
  119.5 3.1 %copy-start.36 = (bf16[12,64,256]{2,1,0:T(8,128)(2,1)S(1)}, bf16[12,64,256]{2,1,0:T(8,128)(2,1)}, u32[]{:S(2)}) copy-start(bf16[12,64,256]{2,1,0:T(8,128)(2,1)} %copy-done.35) | copy-start | bytes 1179652
  119.5 6.6 %slice-start.3 = ((s8[4718592]{0:T(1024)(128)(4,1)}), s8[524288]{0:T(1024)(128)(4,1)S(1)}, s32[]{:S(2)}) async-start(s8[4718592]{0:T(1024)(128)(4,1)} %bitcast.67), calls=%async_computation.3 | async-start | bytes 1048576
  122.6 1.2 copy-start.28
  123.0 1.6 copy-start.5
  126.0 1.3 copy-start.26
  127.9 2.6 copy-start.15
  130.6 6.2 %copy-start.65 = (bf16[768]{0:T(1024)(128)(2,1)S(1)}, bf16[768]{0:T(1024)(128)(2,1)}, u32[]{:S(2)}) copy-start(bf16[768]{0:T(1024)(128)(2,1)} %get-tuple-element.20) | copy-start | bytes 4612
  131.7 17.2 %collective-permute-start.2 = (bf16[64,1536]{0,1:T(8,128)(2,1)}, bf16[64,1536]{0,1:T(8,128)(2,1)}, u32[]{:S(2)}, u32[]{:S(2)}) collective-permute-start(bf16[64,1536]{0,1:T(8,128)(2,1)} %get-tuple-element.53), channel_id=1, source_target_pairs={{0,1},{1,2},{2,3},{3,4},{4,5},{5,6},{6,7},{7,8},{8,9},{9,10},{10,1... | collective-permute-start | bytes 589832 | tf_op jit(solution)/shard_map/ppermute | solution.py:30
  135.5 18.2 %collective-permute-start.3 = (bf16[64,1536]{0,1:T(8,128)(2,1)}, bf16[64,1536]{0,1:T(8,128)(2,1)}, u32[]{:S(2)}, u32[]{:S(2)}) collective-permute-start(bf16[64,1536]{0,1:T(8,128)(2,1)} %get-tuple-element.52), channel_id=1, source_target_pairs={{1,0},{2,1},{3,2},{4,3},{5,4},{6,5},{7,6},{8,7},{9,8},{10,9},{11,1... | collective-permute-start | bytes 589832 | tf_op jit(solution)/shard_map/ppermute | solution.py:32
  158.2 1.5 copy-start.14
  158.2 1.9 copy-start.16
  158.2 1.9 copy-start.64
  161.6 1.1 copy-start.32
  161.6 1.2 copy-start.37
  161.6 1.3 copy-start.38
  161.6 1.3 copy-start.40
  161.6 1.3 copy-start.45
  163.0 2.0 copy-start.1
  163.0 2.0 copy-start.50
  163.0 2.0 copy-start.54
  165.0 1.2 copy-start.58
  166.2 3.1 %copy-start.30 = (f32[256,768]{1,0:T(8,128)}, f32[256,768]{1,0:T(8,128)S(1)}, u32[]{:S(2)}) copy-start(f32[256,768]{1,0:T(8,128)S(1)} %get-tuple-element.81) | copy-start | bytes 2359300
  166.2 3.1 %copy-start.60 = (f32[256]{0:T(256)S(1)}, f32[256]{0:T(256)}, u32[]{:S(2)}) copy-start(f32[256]{0:T(256)} %copy-done.59) | copy-start | bytes 3076
  290.5 2.0 copy-start.18
  290.5 2.0 copy-start.29
  290.5 2.3 copy-start.31
  290.5 2.3 copy-start.62
  (11 other events, 10.3 us)

commit v3 on v1

--- a/solution.py
+++ b/solution.py
@@ -92,7 +92,7 @@
 def gather_kernel(shards, splits, *refs):
     count = len(splits)
     sources, fulls = refs[:count], refs[count : 2 * count]
-    send_sem, recv_sem = refs[2 * count :]
+    keep_sem, send_sem, recv_sem = refs[2 * count :]
     replica = lax.axis_index("replica")
     me = lax.axis_index("shard")
     core = lax.rem(replica, 2)
@@ -138,8 +138,11 @@
                 (replica, lax.rem(me + off, shards)),
             )
             copies[which, off, 0].start()
+    keeps = []
     for which in range(count):
-        fulls[which][me] = sources[which][...]
+        keep = pltpu.make_async_copy(sources[which], fulls[which].at[me], keep_sem.at[which])
+        keep.start()
+        keeps.append(keep)
 
     def forward(which):
         by_rows, by_cols = splits[which]
@@ -175,6 +178,8 @@
             for kind in (2, 3):
                 if (which, off, kind) in copies:
                     copies[which, off, kind].wait_recv()
+    for keep in keeps:
+        keep.wait()
     for one in copies.values():
         one.wait_send()
 
@@ -188,9 +193,10 @@
     fulls = pl.pallas_call(
         functools.partial(gather_kernel, shards, splits),
         out_shape=[jax.ShapeDtypeStruct((shards,) + w.shape, w.dtype) for w in weights],
-        in_specs=[pl.BlockSpec(memory_space=pltpu.VMEM)] * count,
+        in_specs=[pl.BlockSpec(memory_space=pltpu.HBM)] * count,
         out_specs=[pl.BlockSpec(memory_space=pltpu.VMEM)] * count,
         scratch_shapes=[
+            pltpu.SemaphoreType.DMA((count,)),
             pltpu.SemaphoreType.DMA((count, shards - 1, 4)),
             pltpu.SemaphoreType.DMA((count, shards - 1, 4)),
         ],

time: 261 us -> 260 us (level)
  no operation moved by 1% of the time
where the time goes in v3:
time: 260 us; the launch traced here: 259 us
  Pallas kernels  134 us (52%)
  local copies, waits for them, and re-layouts  35.9 us (14%)
  other arithmetic  31 us (12%)
  matrix products  29.9 us (12%)
  waiting for transfers between devices  19.5 us (8%)
  starting transfers between devices  7.26 us (3%)
    pallas_call x1, Pallas kernels, sum_grads(): pl.pallas_call(functools.partial(reduce_kernel, shards, depth, chunks, ro...  88 us
    pallas_call x1, Pallas kernels, gather_weights(): pl.pallas_call(functools.partial(gather_kernel, shards, splits), out_shap...  46.3 us
    unnamed x124, local copies, waits for them, and re-layouts  19 us
    ppermute x2, waiting for transfers between devices, extended(): lax.ppermute(tail, axis, [(i, (i + 1) % count) for i in range(ends)])  9.88 us
    ppermute x2, waiting for transfers between devices, extended(): lax.ppermute(head, axis, [((i + 1) % count, i) for i in range(ends)])  9.58 us
  transfers between devices with their start and end apart: 4, of which 3 were waited for; matrix products, arithmetic and copies ran while one was open for 3% of the time, Pallas kernels for 0%

profile of v3, /device:TPU:0, one launch (start us, length us, event | category | flops | bytes accessed | tf_op | source)
XLA Modules:
  0.0 259.3 jit_solution(13445387965496817426)
XLA Ops:
  0.6 0.7 pad_maximum_fusion.11
  1.4 1.5 copy-done.2
  2.9 1.5 copy-done.3
  4.3 1.2 copy-done.7
  5.5 1.1 copy-done.8
  6.6 46.3 %gather_weights.1 = (bf16[2,16,768]{2,1,0:T(8,128)(2,1)S(1)}, bf16[2,384,2304]{2,1,0:T(8,128)(2,1)S(1)}, bf16[2,384,768]{2,1,0:T(8,128)(2,1)S(1)}, bf16[2,384,2304]{2,1,0:T(8,128)(2,1)}, bf16[2,576,768]{2,1,0:T(8,128)(2,1)S(1)}) custom-call(bf16[16,768]{1,0:T(8,128)(2,1)S(1)} %pad.20.refs_0_, bf16[384,2304]{1,0:T(8,128)(2,1)S(1)} %copy-done.2, ...), custom_call_target="tpu_custom_call" | custom-call | tf_op jit(solution)/shard_map/gather_weights/pallas_call | solution.py:193
  52.9 1.8 copy-done
  54.7 1.2 copy-done.4
  56.4 3.1 %fusion.52 = f32[256,2304]{1,0:T(8,128)S(1)} fusion(bf16[768,2304]{1,0:T(8,128)(2,1)} %bitcast.61, bf16[256,768]{1,0:T(8,128)(2,1)S(1)} %copy-done.12, f32[768]{0:T(1024)S(1)} %reshape.361, f32[256]{0:T(256)S(1)} %fusion.45, f32[256]{0:T(256)S(1)} %broadcast_multiply_fusion.6), kind=kOutput, calls=%fused_computation.140 | convolution fusion | flops 906952704 | bytes 6296576 | tf_op jit(solution)/shard_map/dot_general | solution.py:466
  59.6 1.0 slice.134
  61.3 1.5 copy.33
  63.6 0.8 broadcast_multiply_fusion.3
  64.5 1.1 copy.34
  65.7 1.1 copy.32
  66.8 2.9 %fusion.59 = (f32[256,768]{1,0:T(8,128)}, bf16[256,768]{1,0:T(8,128)(2,1)S(1)}) fusion(f32[256,2304]{1,0:T(8,128)} %copy-done.14, f32[256,768]{1,0:T(8,128)} %copy.34, f32[256,768]{1,0:T(8,128)} %copy.32), kind=kLoop, calls=%fused_computation.145 | loop fusion | flops 589824 | bytes 4325376 | tf_op jit(solution)/shard_map/slice | solution.py:468
  69.7 0.8 pad_maximum_fusion.9
  70.5 2.5 collective-permute-start
  73.0 1.3 collective-permute-start.1
  74.3 1.4 copy.36
  75.7 0.8 slice_negate_fusion.2
  76.6 1.9 fusion.29
  79.4 4.7 %collective-permute-done.1 = bf16[64,1536]{1,0:T(8,128)(2,1)} collective-permute-done((bf16[64,1536]{1,0:T(8,128)(2,1)}, bf16[64,1536]{1,0:T(8,128)(2,1)}, u32[]{:S(2)}, u32[]{:S(2)}) %collective-permute-start.1) | collective-permute-done | bytes 196640 | tf_op jit(solution)/shard_map/ppermute | solution.py:32
  84.1 1.2 pad_maximum_fusion.1
  85.3 0.9 fusion.62
  86.5 1.6 copy.35
  88.1 1.0 fusion.65
  89.2 1.5 fusion
  91.3 1.7 fusion.10
  94.0 1.4 copy-done.25
  95.4 1.1 fusion.55
  97.0 3.1 %add_convert_fusion = (bf16[256,1152]{1,0:T(8,128)(2,1)S(1)}, f32[256,1152]{1,0:T(8,128)S(1)}, f32[256,1152]{1,0:T(8,128)S(1)}) fusion(f32[256,2304]{1,0:T(8,128)S(1)} %fusion.55, bf16[1152,768]{1,0:T(8,128)(2,1)S(1)} %bitcast.63, bf16[256,768]{1,0:T(8,128)(2,1)S(1)} %copy-done.28), kind=kOutput, calls=%fused_computation.45 | convolution fusion | flops 474513408 | bytes 7471104 | tf_op jit(solution)/shard_map/td,fd->tf/dot_general | solution.py:501
  100.1 1.1 multiply_convert_fusion.1
  101.1 1.2 multiply_reduce_fusion.1
  102.9 0.7 copy-done.19
  104.4 3.7 %multiply_reduce_fusion = (f32[12,256]{1,0:T(8,128)S(1)}, f32[12,256,384]{2,1,0:T(8,128)S(1)}) fusion(f32[12,256,384]{2,1,0:T(8,128)} %copy-done.9, f32[12,256]{1,0:T(8,128)S(1)} %log_add_fusion, bf16[256,12,64]{0,2,1:T(8,128)(2,1)S(1)} %bitcast.78, bf16[384,12,64]{0,2,1:T(8,128)(2,1)} %bitcast.87), kind=kOutput, calls=%fused_computation.3 | convolution fusion | flops 154530816 | bytes 10444800 | tf_op jit(solution)/shard_map/qhd,khd->hqk/dot_general | solution.py:531
  108.2 1.4 fusion.3
  109.6 3.1 %convolution_convert_fusion = bf16[768,2304]{1,0:T(8,128)(2,1)} fusion(bf16[256,1152]{1,0:T(8,128)(2,1)S(1)} %get-tuple-element.37, bf16[256,1152]{1,0:T(8,128)(2,1)S(1)} %copy-done.44, f32[256,768]{1,0:T(8,128)S(1)} %copy-done.11, f32[768]{0:T(1024)S(1)} %copy-done.48, f32[256]{0:T(256)S(1)} %fusion.46, f32[256]{0:T(256)S(1)} %broadcast_multiply_fusion.5), kind=kOutput, calls=%fused_computation | convolution fusion | flops 910884864 | bytes 5510144 | tf_op jit(solution)/shard_map/td,tf->df/dot_general | solution.py:504
  113.8 0.7 convolution_convert_fusion.2
  114.5 0.8 copy-done.6
  115.3 1.4 fusion.9
  116.7 1.1 multiply_convert_fusion
  119.0 2.0 broadcast_multiply_fusion
  121.1 1.0 fusion.61
  122.1 2.2 collective-permute-start.2
  124.3 1.3 collective-permute-start.3
  125.6 2.1 fusion.63
  127.7 9.9 %collective-permute-done.2 = bf16[64,1536]{0,1:T(8,128)(2,1)} collective-permute-done((bf16[64,1536]{0,1:T(8,128)(2,1)}, bf16[64,1536]{0,1:T(8,128)(2,1)}, u32[]{:S(2)}, u32[]{:S(2)}) %collective-permute-start.2) | collective-permute-done | bytes 196640 | tf_op jit(solution)/shard_map/ppermute | solution.py:30
  137.5 4.8 %collective-permute-done.3 = bf16[64,1536]{0,1:T(8,128)(2,1)} collective-permute-done((bf16[64,1536]{0,1:T(8,128)(2,1)S(1)}, bf16[64,1536]{0,1:T(8,128)(2,1)}, u32[]{:S(2)}, u32[]{:S(2)}) %collective-permute-start.3) | collective-permute-done | bytes 196640 | tf_op jit(solution)/shard_map/ppermute | solution.py:32
  142.4 0.8 broadcast_in_dim.58
  143.2 3.6 %concatenate.69 = bf16[384,1536]{0,1:T(8,128)(2,1)} concatenate(bf16[64,1536]{0,1:T(8,128)(2,1)} %collective-permute-done.2, bf16[64,1536]{0,1:T(8,128)(2,1)S(1)} %get-tuple-element.43, bf16[128,1536]{0,1:T(8,128)(2,1)} %broadcast_in_dim.58, bf16[64,1536]{0,1:T(8,128)(2,1)} %get-tuple-element.44, bf16[64,1536]{0,1:T(8,128)(2,1)} %collective-permute-done.3), dimensions={0} | concatenate | bytes 2359296 | tf_op jit(solution)/shard_map/concatenate | solution.py:28
  146.8 1.5 fusion.60
  148.7 0.7 fusion.8
  149.5 0.7 copy-done.42
  150.4 1.0 copy-done.33
  152.0 1.6 copy-done.1
  153.7 1.2 fusion.27
  155.0 3.1 %convolution_convert_fusion.1 = bf16[768,2304]{1,0:T(8,128)(2,1)} fusion(bf16[256,768]{0,1:T(8,128)(2,1)S(1)} %slice.188, bf16[256,768]{0,1:T(8,128)(2,1)S(1)} %bitcast.91, bf16[256,768]{0,1:T(8,128)(2,1)S(1)} %bitcast.93, bf16[256,768]{1,0:T(8,128)(2,1)S(1)} %copy-done.13, f32[768]{0:T(1024)S(1)} %copy-done.50, f32[256]{0:T(256)S(1)} %copy-done.54, ...), kind=kOutput, calls=%fused_computation.1 | convolution fusion | flops 912261120 | bytes 5116928 | tf_op jit(solution)/shard_map/td,te->de/dot_general | solution.py:560
  158.6 88.0 %reduce_terms.1 = bf16[3328,768]{1,0:T(8,128)(2,1)} custom-call(bf16[2,384,2304]{2,1,0:T(8,128)(2,1)} %bitcast.80, bf16[2,384,768]{2,1,0:T(8,128)(2,1)S(1)} %bitcast.58, bf16[2,384,2304]{2,1,0:T(8,128)(2,1)} %bitcast.67, bf16[2,576,768]{2,1,0:T(8,128)(2,1)S(1)} %bitcast.57, bf16[2,16,768]{2,1,0:T(8,128)(2,1)S(1)} %fusion.42.refs_4_), custom_call_target="tpu_custom_call" | custom-call | tf_op jit(solution)/shard_map/reduce_terms/pallas_call | solution.py:400
  246.5 3.5 %fusion.58 = (bf16[384,768]{1,0:T(8,128)(2,1)S(1)}, bf16[384,768]{1,0:T(8,128)(2,1)S(1)}, bf16[384,768]{1,0:T(8,128)(2,1)S(1)}, f32[384,768]{1,0:T(8,128)}, bf16...) fusion(bf16[3328,768]{1,0:T(8,128)(2,1)} %reduce_terms.1), kind=kLoop, calls=%fused_computation.144 | loop fusion | flops 294912 | bytes 8847360 | tf_op jit(solution)/shard_map/slice | solution.py:425
  250.0 2.6 %slice_convert_fusion = f32[576,768]{1,0:T(8,128)} fusion(bf16[3328,768]{1,0:T(8,128)(2,1)} %reduce_terms.1), kind=kLoop, calls=%fused_computation.64 | loop fusion | flops 442368 | bytes 2654208 | tf_op jit(solution)/shard_map/convert_element_type | solution.py:425
  252.6 1.3 convert_reduce_fusion.3
  254.0 1.3 add_add_fusion.2
  255.2 2.0 maximum_convert_fusion.1
  257.2 2.0 maximum_convert_fusion
  (162 shorter events, 10.7 us)
Async XLA Ops:
  1.4 1.5 copy-start.2
  2.9 1.5 copy-start.3
  4.3 1.2 copy-start.7
  5.5 1.1 copy-start.8
  6.6 49.4 %copy-start.12 = (bf16[256,768]{1,0:T(8,128)(2,1)S(1)}, bf16[256,768]{1,0:T(8,128)(2,1)}, u32[]{:S(2)}) copy-start(bf16[256,768]{1,0:T(8,128)(2,1)} %param.10) | copy-start | bytes 1179652
  52.9 1.8 copy-start
  54.7 1.2 copy-start.4
  55.9 3.6 %copy-start.49 = (f32[768]{0:T(1024)}, f32[768]{0:T(1024)S(1)}, u32[]{:S(2)}) copy-start(f32[768]{0:T(1024)S(1)} %reshape.361) | copy-start | bytes 9220
  56.1 3.5 %copy-start.51 = (f32[256]{0:T(256)}, f32[256]{0:T(256)S(1)}, u32[]{:S(2)}) copy-start(f32[256]{0:T(256)S(1)} %broadcast_multiply_fusion.6) | copy-start | bytes 3076
  56.3 3.2 %copy-start.55 = (f32[256]{0:T(256)}, f32[256]{0:T(256)S(1)}, u32[]{:S(2)}) copy-start(f32[256]{0:T(256)S(1)} %fusion.26) | copy-start | bytes 3076
  56.4 3.2 %copy-start.53 = (f32[256]{0:T(256)}, f32[256]{0:T(256)S(1)}, u32[]{:S(2)}) copy-start(f32[256]{0:T(256)S(1)} %fusion.45) | copy-start | bytes 3076
  59.6 1.7 copy-start.14
  61.3 8.4 %copy-start.24 = (bf16[256,768]{1,0:T(8,128)(2,1)}, bf16[256,768]{1,0:T(8,128)(2,1)S(1)}, u32[]{:S(2)}) copy-start(bf16[256,768]{1,0:T(8,128)(2,1)S(1)} %slice.189) | copy-start | bytes 1179652
  64.4 12.2 %copy-start.39 = (f32[256,64]{0,1:T(8,128)}, f32[256,64]{0,1:T(8,128)S(1)}, u32[]{:S(2)}) copy-start(f32[256,64]{0,1:T(8,128)S(1)} %get-tuple-element.60) | copy-start | bytes 196612
  64.4 12.2 %copy-start.41 = (f32[256,64]{0,1:T(8,128)}, f32[256,64]{0,1:T(8,128)S(1)}, u32[]{:S(2)}) copy-start(f32[256,64]{0,1:T(8,128)S(1)} %get-tuple-element.59) | copy-start | bytes 196612
  70.5 8.9 %collective-permute-start = (bf16[64,1536]{1,0:T(8,128)(2,1)}, bf16[64,1536]{1,0:T(8,128)(2,1)S(1)}, u32[]{:S(2)}, u32[]{:S(2)}) collective-permute-start(bf16[64,1536]{1,0:T(8,128)(2,1)} %get-tuple-element.53), channel_id=1, source_target_pairs={{0,1},{1,2},{2,3},{3,4},{4,5},{5,6},{6,7},{7,8},{8,9},{9,10},{10,1... | collective-permute-start | bytes 589832 | tf_op jit(solution)/shard_map/ppermute | solution.py:30
  73.0 11.1 %collective-permute-start.1 = (bf16[64,1536]{1,0:T(8,128)(2,1)}, bf16[64,1536]{1,0:T(8,128)(2,1)}, u32[]{:S(2)}, u32[]{:S(2)}) collective-permute-start(bf16[64,1536]{1,0:T(8,128)(2,1)} %get-tuple-element.54), channel_id=1, source_target_pairs={{1,0},{2,1},{3,2},{4,3},{5,4},{6,5},{7,6},{8,7},{9,8},{10,9},{11,1... | collective-permute-start | bytes 589832 | tf_op jit(solution)/shard_map/ppermute | solution.py:32
  76.5 2.6 copy-start.59
  76.5 17.4 %copy-start.47 = (f32[768]{0:T(1024)}, f32[768]{0:T(1024)S(1)}, u32[]{:S(2)}) copy-start(f32[768]{0:T(1024)S(1)} %reshape.362) | copy-start | bytes 9220
  86.2 1.9 copy-start.26
  86.5 2.6 %copy-start.22 = (bf16[384,768]{0,1:T(8,128)(2,1)}, bf16[384,768]{0,1:T(8,128)(2,1)S(1)}, u32[]{:S(2)}) copy-start(bf16[384,768]{0,1:T(8,128)(2,1)S(1)} %copy.37) | copy-start | bytes 1769476
  88.1 2.6 copy-start.34
  89.1 2.1 copy-start.9
  93.0 2.4 copy-start.25
  93.7 8.6 %copy-start.10 = (f32[256,768]{1,0:T(8,128)}, f32[256,768]{1,0:T(8,128)S(1)}, u32[]{:S(2)}) copy-start(f32[256,768]{1,0:T(8,128)S(1)} %get-tuple-element.64) | copy-start | bytes 2359300
  95.4 1.5 copy-start.5
  95.4 1.5 copy-start.28
  100.0 1.1 copy-start.43
  100.0 1.1 copy-start.48
  102.7 0.9 copy-start.19
  104.2 4.0 %slice-start = ((s8[4718592]{0:T(1024)(128)(4,1)}), s8[524288]{0:T(1024)(128)(4,1)S(1)}, s32[]{:S(2)}) async-start(s8[4718592]{0:T(1024)(128)(4,1)} %bitcast.65), calls=%async_computation | async-start | bytes 1048576
  104.3 3.8 %slice-start.1 = ((s8[4718592]{0:T(1024)(128)(4,1)}), s8[4194304]{0:T(1024)(128)(4,1)S(1)}, s32[]{:S(2)}) async-start(s8[4718592]{0:T(1024)(128)(4,1)} %bitcast.65), calls=%async_computation.1 | async-start | bytes 8388608
  108.2 1.4 copy-start.11
  108.2 1.4 copy-start.44
  109.6 11.4 %copy-start.15 = (f32[12,64,384]{2,1,0:T(8,128)}, f32[12,64,384]{2,1,0:T(8,128)S(1)}, u32[]{:S(2)}) copy-start(f32[12,64,384]{2,1,0:T(8,128)S(1)} %fusion.3) | copy-start | bytes 3538948
  109.6 3.1 %copy-start.36 = (bf16[12,64,256]{2,1,0:T(8,128)(2,1)S(1)}, bf16[12,64,256]{2,1,0:T(8,128)(2,1)}, u32[]{:S(2)}) copy-start(bf16[12,64,256]{2,1,0:T(8,128)(2,1)} %copy-done.35) | copy-start | bytes 1179652
  112.6 1.1 copy-start.21
  112.6 1.2 copy-start.29
  113.8 1.5 copy-start.6
  116.7 1.1 copy-start.27
  117.9 1.1 copy-start.23
  117.9 1.1 copy-start.46
  118.4 2.6 %copy-start.17 = (f32[12,64,384]{2,1,0:T(8,128)}, f32[12,64,384]{2,1,0:T(8,128)S(1)}, u32[]{:S(2)}) copy-start(f32[12,64,384]{2,1,0:T(8,128)S(1)} %convolution_multiply_fusion) | copy-start | bytes 3538948
  122.1 15.5 %collective-permute-start.2 = (bf16[64,1536]{0,1:T(8,128)(2,1)}, bf16[64,1536]{0,1:T(8,128)(2,1)}, u32[]{:S(2)}, u32[]{:S(2)}) collective-permute-start(bf16[64,1536]{0,1:T(8,128)(2,1)} %get-tuple-element.44), channel_id=1, source_target_pairs={{0,1},{1,2},{2,3},{3,4},{4,5},{5,6},{6,7},{7,8},{8,9},{9,10},{10,1... | collective-permute-start | bytes 589832 | tf_op jit(solution)/shard_map/ppermute | solution.py:30
  124.3 18.1 %collective-permute-start.3 = (bf16[64,1536]{0,1:T(8,128)(2,1)S(1)}, bf16[64,1536]{0,1:T(8,128)(2,1)}, u32[]{:S(2)}, u32[]{:S(2)}) collective-permute-start(bf16[64,1536]{0,1:T(8,128)(2,1)S(1)} %get-tuple-element.43), channel_id=1, source_target_pairs={{1,0},{2,1},{3,2},{4,3},{5,4},{6,5},{7,6},{8,7},{9,8},{10,9},{11,1... | collective-permute-start | bytes 589832 | tf_op jit(solution)/shard_map/ppermute | solution.py:32
  146.8 1.5 copy-start.16
  146.8 1.9 copy-start.18
  146.8 1.9 copy-start.58
  149.4 0.8 copy-start.42
  149.4 1.0 copy-start.40
  149.4 1.0 copy-start.45
  150.3 1.1 copy-start.33
  150.3 1.2 copy-start.37
  150.3 1.3 copy-start.38
  151.6 2.0 copy-start.1
  151.6 2.1 copy-start.13
  151.6 2.1 copy-start.50
  151.7 2.1 copy-start.52
  153.7 1.2 copy-start.54
  154.9 3.1 %copy-start.31 = (f32[256,768]{1,0:T(8,128)}, f32[256,768]{1,0:T(8,128)S(1)}, u32[]{:S(2)}) copy-start(f32[256,768]{1,0:T(8,128)S(1)} %get-tuple-element.72) | copy-start | bytes 2359300
  155.0 3.1 %copy-start.56 = (f32[256]{0:T(256)S(1)}, f32[256]{0:T(256)}, u32[]{:S(2)}) copy-start(f32[256]{0:T(256)} %copy-done.55) | copy-start | bytes 3076
  250.0 4.0 %copy-start.20 = (f32[256,768]{1,0:T(8,128)S(1)}, f32[256,768]{1,0:T(8,128)}, u32[]{:S(2)}) copy-start(f32[256,768]{1,0:T(8,128)} %copy-done.19) | copy-start | bytes 2359300
  250.0 4.0 %copy-start.30 = (bf16[256,768]{1,0:T(8,128)(2,1)S(1)}, bf16[256,768]{1,0:T(8,128)(2,1)}, u32[]{:S(2)}) copy-start(bf16[256,768]{1,0:T(8,128)(2,1)} %param.11) | copy-start | bytes 1179652
  250.0 4.0 %copy-start.32 = (f32[256,768]{1,0:T(8,128)S(1)}, f32[256,768]{1,0:T(8,128)}, u32[]{:S(2)}) copy-start(f32[256,768]{1,0:T(8,128)} %copy-done.31) | copy-start | bytes 2359300
  (2 other events, 1.4 us)
